TPU v7x, 256 devices: a whole 4x4x8 slice. The times are simulated.
256 devices in a mesh: space: 64 (over x, z, core), dp: 4 (over y).
Axes of the slice: x: 4, y: 4, z: 8, core: 2. Of those that a mesh axis runs over, the one named last changes fastest.
Arguments:
- volume: bfloat16 [4, 64, 32, 8, 256], P('dp', 'space'), may hold values from -6 to 6
- tissue_kept: int32 [4, 64, 4], P('dp', 'space'), may hold values from 0 to 1, as said below
- filter_one: bfloat16 [864, 32], P('dp'), may hold values from -0.21875 to 0.21875
- filter_two: bfloat16 [864, 32], P('dp'), may hold values from -0.21875 to 0.21875
- cotangent: bfloat16 [4, 64, 32, 8, 256], P('dp', 'space'), may hold values from -6 to 6
Outputs:
- activations: bfloat16 [4, 64, 32, 8, 256], P('dp', 'space')
- input_grad: bfloat16 [4, 64, 32, 8, 256], P('dp', 'space')
- filter_grad_one: float32 [864, 32], P('dp')
- filter_grad_two: float32 [864, 32], P('dp')
Inputs may be any that keep to these rules, and one draw needn't show every extreme that they name: tissue_kept[s, d, b] is 1 exactly when the block at x = d // 4 lies below the tissue height of its column, the column of y block 2 * ((d // 2) % 2) + b // 2 and z block 2 * (d % 2) + b % 2; each slab has 16 columns with heights of 1 to 16 blocks, the column of y block 3 and z block 3 of height 16, at least one other column under 16.
All inputs are finite; a program needn't handle non-finite values.
Results may differ from a plain program's by a relative error of at most 0.014.
Values may be sent and summed in bfloat16 or wider, within the bound.
A program may use at most 64 MiB of HBM per device.

v0:
```python
import math

import jax
import jax.numpy as jnp
from jax import lax
from jax.sharding import PartitionSpec as P

NUMBERS = ("NCDHW", "DHWIO", "NCDHW")
GRAD_NUMBERS = ("CNDHW", "IODHW", "NCDHW")


def from_behind(value, axis, steps):
    count = lax.axis_size(axis)
    first, last = (max(0, -steps), min(count, count - steps))
    return lax.ppermute(value, axis, [(source, source + steps) for source in range(first, last)])


def silu_slope(values):
    logistic = jax.nn.sigmoid(values)
    return logistic + values * logistic * (1.0 - logistic)


def correlate(padded, kernel):
    return lax.conv_general_dilated(
        padded[None],
        kernel,
        (1, 1, 1),
        "VALID",
        dimension_numbers=NUMBERS,
        preferred_element_type=jnp.float32,
    )[0]


def flip_kernel(kernel):
    return kernel[::-1, ::-1, ::-1].transpose(0, 1, 2, 4, 3)


def weight_grad(padded, gradient):
    result = lax.conv_general_dilated(
        padded[None],
        gradient[None],
        (1, 1, 1),
        "VALID",
        dimension_numbers=GRAD_NUMBERS,
        preferred_element_type=jnp.float32,
    )
    channels = gradient.shape[0]
    return result.transpose(2, 3, 4, 0, 1).reshape(27 * channels, channels)


def sectioned_halo(tensor, coords, limits):
    widened = tensor
    for axis_dim, stride, place_now, limit_now in (
        (1, 4, coords[0], limits[0]),
        (2, 2, coords[1], limits[1]),
        (3, 1, coords[2], limits[2]),
    ):
        size_now = widened.shape[axis_dim]
        halves = []
        for toward in (stride, -stride):
            if toward > 0:
                outgoing = lax.slice_in_dim(widened, size_now - 1, size_now, axis=axis_dim)
                inside = place_now > 0
            else:
                outgoing = lax.slice_in_dim(widened, 0, 1, axis=axis_dim)
                inside = place_now < limit_now - 1
            arrived = from_behind(outgoing.reshape(-1), "space", toward).reshape(outgoing.shape)
            halves.append(jnp.where(inside, arrived, jnp.zeros_like(arrived)))
        widened = jnp.concatenate((halves[0], widened, halves[1]), axis=axis_dim)
    return widened


def on_device(volume, tissue_kept, filter_one, filter_two, cotangent):
    channels = volume.shape[2]
    thickness = volume.shape[3]
    span_yz = 2 * thickness
    region = lax.axis_index("space")
    coords = (region // 4, region // 2 % 2, region % 2)
    limits = (lax.axis_size("space") // 4, 2, 2)
    block_flags = tissue_kept[0, 0].reshape(2, 2).astype(jnp.float32)
    cell_mask = jnp.broadcast_to(
        block_flags[None, :, None, :, None], (thickness, 2, thickness, 2, thickness)
    ).reshape(thickness, span_yz, span_yz)
    full_one, full_two = (
        lax.all_gather(filter_one, "dp", axis=0, tiled=True),
        lax.all_gather(filter_two, "dp", axis=0, tiled=True),
    )
    kernel_one = full_one.reshape(3, 3, 3, channels, channels)
    kernel_two = full_two.reshape(3, 3, 3, channels, channels)

    def extend(tensor):
        widened = sectioned_halo(tensor, coords, limits)
        return widened

    source = (volume[0, 0].reshape(channels, thickness, span_yz, span_yz) * cell_mask).astype(
        jnp.bfloat16
    )
    padded_source = extend(source)
    pre_one = correlate(padded_source, kernel_one)
    act_one = (jax.nn.silu(pre_one) * cell_mask).astype(jnp.bfloat16)
    padded_act = extend(act_one)
    pre_two = correlate(padded_act, kernel_two)
    output = (jax.nn.silu(pre_two) * cell_mask).astype(jnp.bfloat16)
    upstream = cotangent[0, 0].reshape(channels, thickness, span_yz, span_yz).astype(jnp.float32)
    grad_two = (upstream * cell_mask * silu_slope(pre_two)).astype(jnp.bfloat16)
    back_one = correlate(extend(grad_two), flip_kernel(kernel_two))
    grad_one = (back_one * cell_mask * silu_slope(pre_one)).astype(jnp.bfloat16)
    back_input = (correlate(extend(grad_one), flip_kernel(kernel_one)) * cell_mask).astype(
        jnp.bfloat16
    )
    grad_scale = 1.0 / math.sqrt(
        lax.axis_size("dp") * lax.axis_size("space") * thickness * span_yz * span_yz
    )
    partials = (
        weight_grad(padded_source, grad_one) * grad_scale,
        weight_grad(padded_act, grad_two) * grad_scale,
    )
    summed = lax.psum((partials[0], partials[1]), "space")
    grad_first, grad_second = (
        lax.psum_scatter(
            summed[0].astype(jnp.bfloat16), "dp", scatter_dimension=0, tiled=True
        ).astype(jnp.float32),
        lax.psum_scatter(
            summed[1].astype(jnp.bfloat16), "dp", scatter_dimension=0, tiled=True
        ).astype(jnp.float32),
    )
    return (output.reshape(volume.shape), back_input.reshape(volume.shape), grad_first, grad_second)


def solution(mesh):
    placed = (
        P("dp", "space", None, None, None),
        P("dp", "space", None),
        P("dp", None),
        P("dp", None),
        P("dp", "space", None, None, None),
    )
    return jax.shard_map(
        on_device,
        mesh=mesh,
        in_specs=placed,
        out_specs=(
            P("dp", "space", None, None, None),
            P("dp", "space", None, None, None),
            P("dp", None),
            P("dp", None),
        ),
        check_vma=False,
    )
```

profile of v0, /device:TPU:2, one launch (start us, length us, event | category | flops | bytes accessed | tf_op | source)
XLA Modules:
  0.0 519.1 jit_solution(342738763406879992)
XLA Ops:
  8.1 1.2 copy.261
  9.8 5.2 collective-permute-start
  15.3 4.9 collective-permute-start.1
  20.6 2.8 collective-permute-done.1
  24.1 2.9 collective-permute-start.2
  27.3 5.0 collective-permute-start.3
  32.7 1.9 collective-permute-done.3
  35.4 1.9 collective-permute-start.4
  37.4 12.4 %all-gather = bf16[4,216,32]{1,2,0:T(8,128)(2,1)S(1)} all-gather(bf16[1,216,32]{1,2,0:T(8,128)(2,1)S(1)} %bitcast.238), channel_id=1, replica_groups=mesh['space'=64,'dp'=4] {'dp'}, dimensions={0}, use_global_device_ids=true | all-gather | bytes 69120 | tf_op jit(solution)/shard_map/all_gather | solution.py:85
  50.3 2.9 collective-permute-start.5
  53.6 1.0 collective-permute-done.5
  55.0 1.7 fusion.96
  58.3 3.7 multiply_add_fusion.1
  62.4 1.0 copy-done
  64.2 3.4 collective-permute-start.6
  67.9 5.5 %collective-permute-start.7 = (bf16[8192]{0:T(1024)(128)(2,1)S(1)}, bf16[8192]{0:T(1024)(128)(2,1)S(1)}, u32[]{:S(2)}, u32[]{:S(2)}) collective-permute-start(bf16[8192]{0:T(1024)(128)(2,1)S(1)} %reshape.563), channel_id=1, source_target_pairs={{16,0},{20,4},{24,8},{28,12},{32,16},{36,20},{40,24},{44,28},{48,3... | collective-permute-start | bytes 49160 | tf_op jit(solution)/shard_map/ppermute | solution.py:15
  73.7 1.1 collective-permute-done.7
  75.5 2.9 collective-permute-start.8
  78.7 5.8 %collective-permute-start.9 = (bf16[5120]{0:T(1024)(128)(2,1)S(1)}, bf16[5120]{0:T(1024)(128)(2,1)S(1)}, u32[]{:S(2)}, u32[]{:S(2)}) collective-permute-start(bf16[5120]{0:T(1024)(128)(2,1)S(1)} %reshape.565), channel_id=1, source_target_pairs={{8,0},{12,4},{16,8},{20,12},{24,16},{28,20},{32,24},{36,28},{40,32... | collective-permute-start | bytes 30728 | tf_op jit(solution)/shard_map/ppermute | solution.py:15
  84.8 1.1 collective-permute-done.9
  86.7 1.9 collective-permute-start.10
  88.6 12.1 %all-gather.1 = bf16[4,216,32]{1,2,0:T(8,128)(2,1)S(1)} all-gather(bf16[1,216,32]{1,2,0:T(8,128)(2,1)S(1)} %bitcast.239), channel_id=1, replica_groups=mesh['space'=64,'dp'=4] {'dp'}, dimensions={0}, use_global_device_ids=true | all-gather | bytes 69120 | tf_op jit(solution)/shard_map/all_gather | solution.py:86
  101.7 2.9 collective-permute-start.11
  105.0 1.0 collective-permute-done.11
  106.4 1.7 fusion.94
  108.1 1.2 pad.2
  109.3 2.8 reshape.590
  112.6 3.7 multiply_add_fusion
  117.5 1.9 collective-permute-start.12
  119.8 6.9 %collective-permute-start.13 = (bf16[8192]{0:T(1024)(128)(2,1)S(1)}, bf16[8192]{0:T(1024)(128)(2,1)S(1)}, u32[]{:S(2)}, u32[]{:S(2)}) collective-permute-start(bf16[8192]{0:T(1024)(128)(2,1)S(1)} %reshape.570), channel_id=1, source_target_pairs={{16,0},{20,4},{24,8},{28,12},{32,16},{36,20},{40,24},{44,28},{48,3... | collective-permute-start | bytes 49160 | tf_op jit(solution)/shard_map/ppermute | solution.py:15
  127.0 1.1 collective-permute-done.13
  128.8 2.4 collective-permute-start.14
  131.5 5.6 %collective-permute-start.15 = (bf16[5120]{0:T(1024)(128)(2,1)S(1)}, bf16[5120]{0:T(1024)(128)(2,1)S(1)}, u32[]{:S(2)}, u32[]{:S(2)}) collective-permute-start(bf16[5120]{0:T(1024)(128)(2,1)S(1)} %reshape.572), channel_id=1, source_target_pairs={{8,0},{12,4},{16,8},{20,12},{24,16},{28,20},{32,24},{36,28},{40,32... | collective-permute-start | bytes 30728 | tf_op jit(solution)/shard_map/ppermute | solution.py:15
  137.3 1.1 collective-permute-done.15
  139.2 1.9 collective-permute-start.16
  143.1 1.7 copy.329
  144.8 1.1 slice.122
  145.9 1.3 copy.346
  147.9 1.1 slice.123
  149.4 5.8 %collective-permute-start.17 = (bf16[5760]{0:T(1024)(128)(2,1)S(1)}, bf16[5760]{0:T(1024)(128)(2,1)S(1)}, u32[]{:S(2)}, u32[]{:S(2)}) collective-permute-start(bf16[5760]{0:T(1024)(128)(2,1)S(1)} %reshape.574), channel_id=1, source_target_pairs={{4,0},{8,4},{12,8},{16,12},{20,16},{24,20},{28,24},{32,28},{36,32}... | collective-permute-start | bytes 34568 | tf_op jit(solution)/shard_map/ppermute | solution.py:15
  155.5 1.0 collective-permute-done.17
  157.6 1.3 pad.4
  158.9 2.8 reshape.597
  162.1 2.4 fusion.39
  164.9 1.1 copy-done.1
  166.0 0.9 fusion.59
  167.3 2.6 collective-permute-start.18
  170.2 15.0 %collective-permute-start.19 = (bf16[8192]{0:T(1024)(128)(2,1)S(1)}, bf16[8192]{0:T(1024)(128)(2,1)S(1)}, u32[]{:S(2)}, u32[]{:S(2)}) collective-permute-start(bf16[8192]{0:T(1024)(128)(2,1)S(1)} %reshape.576), channel_id=1, source_target_pairs={{16,0},{20,4},{24,8},{28,12},{32,16},{36,20},{40,24},{44,28},{48,3... | collective-permute-start | bytes 49160 | tf_op jit(solution)/shard_map/ppermute | solution.py:15
  185.2 3.0 fusion.55
  188.3 11.2 %fusion.48 = f32[3,3,3,32,32]{4,3,2,1,0:T(8,128)S(1)} fusion(bf16[1,32,10,18,18]{1,4,3,2,0:T(8,128)(2,1)S(1)} %copy-done.4, bf16[1,32,8,16,16]{1,4,3,2,0:T(8,128)(2,1)S(1)} %get-tuple-element.53), kind=kOutput, calls=%fused_computation.39 | convolution fusion | flops 113273856 | bytes 449024 | tf_op jit(solution)/shard_map/transpose | solution.py:48
  200.7 1.9 collective-permute-start.20
  202.6 11.8 %fusion.51 = f32[3,3,3,32,32]{4,3,2,1,0:T(8,128)} fusion(bf16[1,32,10,18,18]{1,4,3,2,0:T(8,128)(2,1)S(1)} %copy-done.5, bf16[1,32,8,16,16]{1,4,3,2,0:T(8,128)(2,1)S(1)} %get-tuple-element.52), kind=kOutput, calls=%fused_computation.40 | convolution fusion | flops 113273856 | bytes 449024 | tf_op jit(solution)/shard_map/transpose | solution.py:48
  214.4 1.2 copy.338
  216.1 6.0 %collective-permute-start.21 = (bf16[5120]{0:T(1024)(128)(2,1)S(1)}, bf16[5120]{0:T(1024)(128)(2,1)S(1)}, u32[]{:S(2)}, u32[]{:S(2)}) collective-permute-start(bf16[5120]{0:T(1024)(128)(2,1)S(1)} %reshape.578), channel_id=1, source_target_pairs={{8,0},{12,4},{16,8},{20,12},{24,16},{28,20},{32,24},{36,28},{40,32... | collective-permute-start | bytes 30728 | tf_op jit(solution)/shard_map/ppermute | solution.py:15
  222.4 1.1 collective-permute-done.21
  224.3 1.9 collective-permute-start.22
  226.3 212.2 %all-reduce.8 = (bf16[864,32]{0,1:T(8,128)(2,1)}, bf16[864,32]{0,1:T(8,128)(2,1)}) all-reduce(f32[864,32]{0,1:T(8,128)S(1)} %copy.333, f32[864,32]{0,1:T(8,128)S(1)} %copy.338), channel_id=1, replica_groups=mesh['space'=64,'dp'=4] {'space'}, use_global_device_ids=true, to_apply=%region_0.1 | all-reduce | flops 55296 | bytes 331776 | tf_op jit(solution)/shard_map/psum | solution.py:118
  438.9 1.9 collective-permute-start.23
  441.2 1.0 collective-permute-done.23
  445.1 2.4 fusion.36
  448.3 0.9 copy-done.2
  449.5 0.9 copy.340
  451.3 59.0 %all-reduce.7.cloned.1.call-done = (bf16[864,32]{0,1:T(8,128)(2,1)}, bf16[864,32]{0,1:T(8,128)(2,1)}) async-done(((bf16[864,32]{0,1:T(8,128)(2,1)}, bf16[864,32]{0,1:T(8,128)(2,1)}), (bf16[864,32]{0,1:T(8,128)(2,1)}, bf16[864,32]{0,1:T(8,128)(2,1)})) %all-reduce.7.cloned.1.call-update) | async-done | bytes 110608
  510.3 1.5 dynamic-slice_convert_fusion
  (214 shorter events, 30.1 us)
Async XLA Ops:
  7.2 503.2 %all-reduce.7.cloned.1.call-start = ((), (), s32[]{:S(2)}) async-start(), calls=%async_computation | async-start | bytes 229376
  9.8 10.4 %collective-permute-start = (bf16[8192]{0:T(1024)(128)(2,1)S(1)}, bf16[8192]{0:T(1024)(128)(2,1)S(1)}, u32[]{:S(2)}, u32[]{:S(2)}) collective-permute-start(bf16[8192]{0:T(1024)(128)(2,1)S(1)} %reshape.555), channel_id=1, source_target_pairs={{0,16},{4,20},{8,24},{12,28},{16,32},{20,36},{24,40},{28,44},{32,4... | collective-permute-start | bytes 49160 | tf_op jit(solution)/shard_map/ppermute | solution.py:15
  15.3 8.1 %collective-permute-start.1 = (bf16[8192]{0:T(1024)(128)(2,1)S(1)}, bf16[8192]{0:T(1024)(128)(2,1)S(1)}, u32[]{:S(2)}, u32[]{:S(2)}) collective-permute-start(bf16[8192]{0:T(1024)(128)(2,1)S(1)} %reshape.556), channel_id=1, source_target_pairs={{16,0},{20,4},{24,8},{28,12},{32,16},{36,20},{40,24},{44,28},{48,3... | collective-permute-start | bytes 49160 | tf_op jit(solution)/shard_map/ppermute | solution.py:15
  23.8 13.6 %copy-start.9 = (bf16[216,32]{0,1:T(8,128)(2,1)S(1)}, bf16[216,32]{0,1:T(8,128)(2,1)}, u32[]{:S(2)}) copy-start(bf16[216,32]{0,1:T(8,128)(2,1)} %param.7) | copy-start | bytes 41476
  24.1 8.3 %collective-permute-start.2 = (bf16[5120]{0:T(1024)(128)(2,1)S(1)}, bf16[5120]{0:T(1024)(128)(2,1)S(1)}, u32[]{:S(2)}, u32[]{:S(2)}) collective-permute-start(bf16[5120]{0:T(1024)(128)(2,1)S(1)} %reshape.557), channel_id=1, source_target_pairs={{0,8},{4,12},{8,16},{12,20},{16,24},{20,28},{24,32},{28,36},{32,40... | collective-permute-start | bytes 30728 | tf_op jit(solution)/shard_map/ppermute | solution.py:15
  27.3 7.2 %collective-permute-start.3 = (bf16[5120]{0:T(1024)(128)(2,1)S(1)}, bf16[5120]{0:T(1024)(128)(2,1)S(1)}, u32[]{:S(2)}, u32[]{:S(2)}) collective-permute-start(bf16[5120]{0:T(1024)(128)(2,1)S(1)} %reshape.558), channel_id=1, source_target_pairs={{8,0},{12,4},{16,8},{20,12},{24,16},{28,20},{32,24},{36,28},{40,32... | collective-permute-start | bytes 30728 | tf_op jit(solution)/shard_map/ppermute | solution.py:15
  35.4 17.8 %collective-permute-start.4 = (bf16[5760]{0:T(1024)(128)(2,1)S(1)}, bf16[5760]{0:T(1024)(128)(2,1)S(1)}, u32[]{:S(2)}, u32[]{:S(2)}) collective-permute-start(bf16[5760]{0:T(1024)(128)(2,1)S(1)} %reshape.559), channel_id=1, source_target_pairs={{0,4},{4,8},{8,12},{12,16},{16,20},{20,24},{24,28},{28,32},{32,36}... | collective-permute-start | bytes 34568 | tf_op jit(solution)/shard_map/ppermute | solution.py:15
  49.9 8.2 %copy-start.6 = (bf16[4,216,32]{2,1,0:T(8,128)(2,1)}, bf16[4,216,32]{2,1,0:T(8,128)(2,1)S(1)}, u32[]{:S(2)}) copy-start(bf16[4,216,32]{2,1,0:T(8,128)(2,1)S(1)} %copy.276) | copy-start | bytes 165892
  50.3 4.3 collective-permute-start.5
  57.7 0.7 copy-start.13
  62.4 1.0 copy-start
  64.2 9.2 %collective-permute-start.6 = (bf16[8192]{0:T(1024)(128)(2,1)S(1)}, bf16[8192]{0:T(1024)(128)(2,1)S(1)}, u32[]{:S(2)}, u32[]{:S(2)}) collective-permute-start(bf16[8192]{0:T(1024)(128)(2,1)S(1)} %reshape.562), channel_id=1, source_target_pairs={{0,16},{4,20},{8,24},{12,28},{16,32},{20,36},{24,40},{28,44},{32,4... | collective-permute-start | bytes 49160 | tf_op jit(solution)/shard_map/ppermute | solution.py:15
  67.9 6.9 %collective-permute-start.7 = (bf16[8192]{0:T(1024)(128)(2,1)S(1)}, bf16[8192]{0:T(1024)(128)(2,1)S(1)}, u32[]{:S(2)}, u32[]{:S(2)}) collective-permute-start(bf16[8192]{0:T(1024)(128)(2,1)S(1)} %reshape.563), channel_id=1, source_target_pairs={{16,0},{20,4},{24,8},{28,12},{32,16},{36,20},{40,24},{44,28},{48,3... | collective-permute-start | bytes 49160 | tf_op jit(solution)/shard_map/ppermute | solution.py:15
  75.1 13.5 %copy-start.10 = (bf16[216,32]{0,1:T(8,128)(2,1)S(1)}, bf16[216,32]{0,1:T(8,128)(2,1)}, u32[]{:S(2)}) copy-start(bf16[216,32]{0,1:T(8,128)(2,1)} %param.8) | copy-start | bytes 41476
  75.1 25.8 %copy-start.8 = (bf16[1,1,32,8,256]{4,3,2,1,0:T(8,128)(2,1)S(1)}, bf16[1,1,32,8,256]{4,3,2,1,0:T(8,128)(2,1)}, u32[]{:S(2)}) copy-start(bf16[1,1,32,8,256]{4,3,2,1,0:T(8,128)(2,1)} %param.9) | copy-start | bytes 393220
  75.5 9.0 %collective-permute-start.8 = (bf16[5120]{0:T(1024)(128)(2,1)S(1)}, bf16[5120]{0:T(1024)(128)(2,1)S(1)}, u32[]{:S(2)}, u32[]{:S(2)}) collective-permute-start(bf16[5120]{0:T(1024)(128)(2,1)S(1)} %reshape.564), channel_id=1, source_target_pairs={{0,8},{4,12},{8,16},{12,20},{16,24},{20,28},{24,32},{28,36},{32,40... | collective-permute-start | bytes 30728 | tf_op jit(solution)/shard_map/ppermute | solution.py:15
  78.7 7.2 %collective-permute-start.9 = (bf16[5120]{0:T(1024)(128)(2,1)S(1)}, bf16[5120]{0:T(1024)(128)(2,1)S(1)}, u32[]{:S(2)}, u32[]{:S(2)}) collective-permute-start(bf16[5120]{0:T(1024)(128)(2,1)S(1)} %reshape.565), channel_id=1, source_target_pairs={{8,0},{12,4},{16,8},{20,12},{24,16},{28,20},{32,24},{36,28},{40,32... | collective-permute-start | bytes 30728 | tf_op jit(solution)/shard_map/ppermute | solution.py:15
  86.7 17.9 %collective-permute-start.10 = (bf16[5760]{0:T(1024)(128)(2,1)S(1)}, bf16[5760]{0:T(1024)(128)(2,1)S(1)}, u32[]{:S(2)}, u32[]{:S(2)}) collective-permute-start(bf16[5760]{0:T(1024)(128)(2,1)S(1)} %reshape.566), channel_id=1, source_target_pairs={{0,4},{4,8},{8,12},{12,16},{16,20},{20,24},{24,28},{28,32},{32,36}... | collective-permute-start | bytes 34568 | tf_op jit(solution)/shard_map/ppermute | solution.py:15
  101.7 4.3 collective-permute-start.11
  117.5 9.2 %collective-permute-start.12 = (bf16[8192]{0:T(1024)(128)(2,1)S(1)}, bf16[8192]{0:T(1024)(128)(2,1)S(1)}, u32[]{:S(2)}, u32[]{:S(2)}) collective-permute-start(bf16[8192]{0:T(1024)(128)(2,1)S(1)} %reshape.569), channel_id=1, source_target_pairs={{0,16},{4,20},{8,24},{12,28},{16,32},{20,36},{24,40},{28,44},{32,4... | collective-permute-start | bytes 49160 | tf_op jit(solution)/shard_map/ppermute | solution.py:15
  119.8 8.4 %collective-permute-start.13 = (bf16[8192]{0:T(1024)(128)(2,1)S(1)}, bf16[8192]{0:T(1024)(128)(2,1)S(1)}, u32[]{:S(2)}, u32[]{:S(2)}) collective-permute-start(bf16[8192]{0:T(1024)(128)(2,1)S(1)} %reshape.570), channel_id=1, source_target_pairs={{16,0},{20,4},{24,8},{28,12},{32,16},{36,20},{40,24},{44,28},{48,3... | collective-permute-start | bytes 49160 | tf_op jit(solution)/shard_map/ppermute | solution.py:15
  128.4 13.4 %copy-start.12 = (u32[256]{0:T(256)S(1)}, u32[256]{0:T(256)}, u32[]{:S(2)}) copy-start(u32[256]{0:T(256)} %constant.84) | copy-start | bytes 3076
  128.8 8.3 %collective-permute-start.14 = (bf16[5120]{0:T(1024)(128)(2,1)S(1)}, bf16[5120]{0:T(1024)(128)(2,1)S(1)}, u32[]{:S(2)}, u32[]{:S(2)}) collective-permute-start(bf16[5120]{0:T(1024)(128)(2,1)S(1)} %reshape.571), channel_id=1, source_target_pairs={{0,8},{4,12},{8,16},{12,20},{16,24},{20,28},{24,32},{28,36},{32,40... | collective-permute-start | bytes 30728 | tf_op jit(solution)/shard_map/ppermute | solution.py:15
  131.5 6.9 %collective-permute-start.15 = (bf16[5120]{0:T(1024)(128)(2,1)S(1)}, bf16[5120]{0:T(1024)(128)(2,1)S(1)}, u32[]{:S(2)}, u32[]{:S(2)}) collective-permute-start(bf16[5120]{0:T(1024)(128)(2,1)S(1)} %reshape.572), channel_id=1, source_target_pairs={{8,0},{12,4},{16,8},{20,12},{24,16},{28,20},{32,24},{36,28},{40,32... | collective-permute-start | bytes 30728 | tf_op jit(solution)/shard_map/ppermute | solution.py:15
  139.2 15.9 %collective-permute-start.16 = (bf16[5760]{0:T(1024)(128)(2,1)S(1)}, bf16[5760]{0:T(1024)(128)(2,1)S(1)}, u32[]{:S(2)}, u32[]{:S(2)}) collective-permute-start(bf16[5760]{0:T(1024)(128)(2,1)S(1)} %reshape.573), channel_id=1, source_target_pairs={{0,4},{4,8},{8,12},{12,16},{16,20},{20,24},{24,28},{28,32},{32,36}... | collective-permute-start | bytes 34568 | tf_op jit(solution)/shard_map/ppermute | solution.py:15
  145.9 1.7 copy-start.3
  149.4 7.1 %collective-permute-start.17 = (bf16[5760]{0:T(1024)(128)(2,1)S(1)}, bf16[5760]{0:T(1024)(128)(2,1)S(1)}, u32[]{:S(2)}, u32[]{:S(2)}) collective-permute-start(bf16[5760]{0:T(1024)(128)(2,1)S(1)} %reshape.574), channel_id=1, source_target_pairs={{4,0},{8,4},{12,8},{16,12},{20,16},{24,20},{28,24},{32,28},{36,32}... | collective-permute-start | bytes 34568 | tf_op jit(solution)/shard_map/ppermute | solution.py:15
  164.8 1.2 copy-start.1
  167.3 32.2 %collective-permute-start.18 = (bf16[8192]{0:T(1024)(128)(2,1)S(1)}, bf16[8192]{0:T(1024)(128)(2,1)S(1)}, u32[]{:S(2)}, u32[]{:S(2)}) collective-permute-start(bf16[8192]{0:T(1024)(128)(2,1)S(1)} %reshape.575), channel_id=1, source_target_pairs={{0,16},{4,20},{8,24},{12,28},{16,32},{20,36},{24,40},{28,44},{32,4... | collective-permute-start | bytes 49160 | tf_op jit(solution)/shard_map/ppermute | solution.py:15
  170.2 29.6 %collective-permute-start.19 = (bf16[8192]{0:T(1024)(128)(2,1)S(1)}, bf16[8192]{0:T(1024)(128)(2,1)S(1)}, u32[]{:S(2)}, u32[]{:S(2)}) collective-permute-start(bf16[8192]{0:T(1024)(128)(2,1)S(1)} %reshape.576), channel_id=1, source_target_pairs={{16,0},{20,4},{24,8},{28,12},{32,16},{36,20},{40,24},{44,28},{48,3... | collective-permute-start | bytes 49160 | tf_op jit(solution)/shard_map/ppermute | solution.py:15
  185.2 3.0 copy-start.4
  199.5 3.1 copy-start.5
  200.7 21.5 %collective-permute-start.20 = (bf16[5120]{0:T(1024)(128)(2,1)S(1)}, bf16[5120]{0:T(1024)(128)(2,1)S(1)}, u32[]{:S(2)}, u32[]{:S(2)}) collective-permute-start(bf16[5120]{0:T(1024)(128)(2,1)S(1)} %reshape.577), channel_id=1, source_target_pairs={{0,8},{4,12},{8,16},{12,20},{16,24},{20,28},{24,32},{28,36},{32,40... | collective-permute-start | bytes 30728 | tf_op jit(solution)/shard_map/ppermute | solution.py:15
  216.1 7.4 %collective-permute-start.21 = (bf16[5120]{0:T(1024)(128)(2,1)S(1)}, bf16[5120]{0:T(1024)(128)(2,1)S(1)}, u32[]{:S(2)}, u32[]{:S(2)}) collective-permute-start(bf16[5120]{0:T(1024)(128)(2,1)S(1)} %reshape.578), channel_id=1, source_target_pairs={{8,0},{12,4},{16,8},{20,12},{24,16},{28,20},{32,24},{36,28},{40,32... | collective-permute-start | bytes 30728 | tf_op jit(solution)/shard_map/ppermute | solution.py:15
  224.3 216.4 %collective-permute-start.22 = (bf16[5760]{0:T(1024)(128)(2,1)S(1)}, bf16[5760]{0:T(1024)(128)(2,1)S(1)}, u32[]{:S(2)}, u32[]{:S(2)}) collective-permute-start(bf16[5760]{0:T(1024)(128)(2,1)S(1)} %reshape.579), channel_id=1, source_target_pairs={{0,4},{4,8},{8,12},{12,16},{16,20},{20,24},{24,28},{28,32},{32,36}... | collective-permute-start | bytes 34568 | tf_op jit(solution)/shard_map/ppermute | solution.py:15
  438.9 3.3 collective-permute-start.23
  444.2 0.9 copy-start.7
  444.2 0.9 copy-start.14
  447.9 1.2 copy-start.2
  447.9 1.2 copy-start.11
Sparse Core Ops, SparseCore 0:
  438.6 71.6 all-reduce.6
where the time goes:
time: 529 us; the launch traced here: 519 us
  blocking collectives  237 us (45%)
  starting transfers between devices  99.2 us (19%)
  waiting for transfers between devices  73 us (14%)
  local copies, waits for them, and re-layouts  45 us (9%)
  matrix products  35.2 us (7%)
  between operations  16.4 us (3%)
  other arithmetic  13.6 us (3%)
    psum x1, blocking collectives, on_device(): summed = lax.psum((partials[0], partials[1]), 'space')  212 us
    ppermute x24, starting transfers between devices, from_behind(): lax.ppermute(value, axis, [(source, source + steps) for source in range(f...  99.1 us
    unnamed x2, waiting for transfers between devices  59.1 us
    transpose x2, matrix products, weight_grad(): return result.transpose(2, 3, 4, 0, 1).reshape(27 * channels, channels)  23 us
    ppermute x24, waiting for transfers between devices, from_behind(): lax.ppermute(value, axis, [(source, source + steps) for source in range(f...  13.9 us
    all_gather x1, blocking collectives, on_device(): lax.all_gather(filter_one, 'dp', axis=0, tiled=True)  12.4 us
    conv_general_dilated x4, matrix products, correlate(): lax.conv_general_dilated(padded[None], kernel, (1, 1, 1), 'VALID', dimens...  12.2 us
    all_gather x1, blocking collectives, on_device(): lax.all_gather(filter_two, 'dp', axis=0, tiled=True)  12.1 us
  transfers between devices with their start and end apart: 25, of which 12 were waited for; matrix products, arithmetic and copies ran while one was open for 10% of the time, Pallas kernels for 0%

commit v1 on v0

v1 whole, which is shorter than its diff:
```python
import functools
import math

import jax
import jax.numpy as jnp
from jax import lax
from jax.experimental import pallas as pl
from jax.experimental.pallas import tpu as pltpu
from jax.sharding import PartitionSpec as P

MESH = pl.DeviceIdType.MESH
F32 = jnp.float32
BF16 = jnp.bfloat16

C = 32
CELLS = 256
ROWS = 256
EXT = 320
DEPTH = 9 * EXT
PAD = 2944
GROUP = 16

NN = (((1,), (0,)), ((), ()))
NT = (((1,), (1,)), ((), ()))


def dot(a, b, dims=NN):
    return lax.dot_general(a, b, dims, preferred_element_type=F32)


def iota(shape, axis):
    return lax.broadcasted_iota(jnp.int32, shape, axis)


def spread(cond):
    return jnp.where(cond, 1.0, 0.0).astype(BF16)


def pick(lane_group, parts):
    value = parts[-1]
    for g in range(len(parts) - 2, -1, -1):
        value = jnp.where(lane_group == g, parts[g], value)
    return value


def kernel(
    kept, filter_one, filter_two, volume, cotangent,
    act_out, gin_out, grad_one_out, grad_two_out,
    vin, cin, vout, own, faces, faces_in, edges_in, ext, beside, halo, shifted, banded,
    wsend, wrecv, wrows, wback, product, pile, scattered, summed, crossed, final, gathered,
    sel, expand, perm, perm_back,
    local_sem, out_sem, halo_send, halo_recv, filt_send, filt_recv,
    rs_send, rs_recv, xy_send, xy_recv, ag_send, ag_recv,
):
    space = lax.axis_index("space")
    dp = lax.axis_index("dp")
    count = lax.axis_size("space")
    rx, ry, rz = space // 4, (space // 2) % 2, space % 2
    block, zc = space // GROUP, space % GROUP
    xy = block * 4 + dp
    has_below, has_above = rx > 0, rx < count // 4 - 1

    loads = [
        pltpu.make_async_copy(volume.at[0, 0], vin, local_sem.at[0]),
        pltpu.make_async_copy(cotangent.at[0, 0], cin, local_sem.at[1]),
    ]
    for load in loads:
        load.start()

    base = space - 2 * ry - rz
    flips = (base + 2 * (1 - ry) + rz, base + 2 * ry + (1 - rz), base + 2 * (1 - ry) + (1 - rz))
    below = [lax.rem(d - 4 + count, count) for d in (space,) + flips]
    above = [lax.rem(d + 4, count) for d in (space,) + flips]
    zc_peers = [block * GROUP + lax.rem(zc + k, GROUP) for k in range(1, GROUP)]
    xy_slots = [lax.rem(xy + k, GROUP) for k in range(1, GROUP)]
    xy_peers = [((s // 4) * GROUP + zc, s % 4) for s in xy_slots]

    barrier = pltpu.get_barrier_semaphore()
    greeted = [(d, dp) for d in zc_peers] + xy_peers + [(d, dp) for d in below + above]
    for peer in greeted:
        pl.semaphore_signal(barrier, inc=1, device_id=peer, device_id_type=MESH)

    group = iota((1, 128), 1) // C
    within = iota((1, 128), 1) % C
    row = iota((CELLS, 128), 0)
    k = iota((CELLS, 128), 1) % C
    yb, zb = 15 * (1 - ry), 15 * (1 - rz)
    sel[...] = spread(((k < 16) & (row == yb * 16 + k)) | ((k >= 16) & (row == (k - 16) * 16 + zb)))

    row = iota((256, 256), 0)
    col = iota((256, 256), 1)
    perm[...] = spread(col == 8 * (row % C) + row // C)
    perm_back[...] = spread(row == 8 * (col % C) + col // C)
    k = row % C
    expand[:, :256] = spread(
        (row < 128) & (k >= 16) & (k - 16 == col // 16) & (col % 16 == 15 * (1 - rz))
    )
    row = iota((256, 128), 0)
    k = row % C
    z = iota((256, 128), 1) - 112 * (1 - ry)
    corner, beyond = 15 * rz, 16 - 17 * rz
    for oz in (-1, 0, 1):
        expand[:, 384 + 128 * oz : 512 + 128 * oz] = spread(
            (z >= 0) & (z < 16)
            & (((row < 128) & (k < 16) & (k == z + oz)) | ((row >= 128) & (k == corner) & (z + oz == beyond)))
        )
    zero = jnp.zeros((256, PAD), BF16)
    for f in range(4):
        banded[f] = zero
        shifted[f, DEPTH:PAD] = zero[: PAD - DEPTH, :CELLS]
    wrows[...] = jnp.zeros(wrows.shape, F32)

    repeat = spread(iota((C, 128), 1) % C == iota((C, 128), 0))
    for f, rows in enumerate((filter_one, filter_two)):
        wide = dot(rows[...], repeat)
        wide = jnp.concatenate([wide, jnp.zeros((8, 128), F32)], axis=0)
        packed = pick(group, [wide[56 * g : 56 * g + 56] for g in range(4)])
        packed = jnp.concatenate([packed, jnp.zeros((8, 128), F32)], axis=0).astype(BF16)
        wsend[f] = packed
        wrecv[f, dp] = packed

    cell = iota((1, CELLS), 1)
    tile = 2 * (cell // 128) + (cell % 16) // 8
    keep = jnp.zeros((1, CELLS), F32)
    for b in range(4):
        keep = jnp.where(tile == b, kept[0, 0, b].astype(F32), keep)

    def arrive(staged):
        return dot(perm[...], staged[...].astype(F32).reshape(ROWS, CELLS).astype(BF16))

    def halo_copies(r):
        peer = lambda d: (d, dp)
        copies = []

        def add(src, dst, d):
            i = len(copies)
            copies.append(
                pltpu.make_async_remote_copy(
                    src_ref=src, dst_ref=dst, send_sem=halo_send.at[r, i], recv_sem=halo_recv.at[r, i],
                    device_id=peer(d), device_id_type=MESH,
                )
            )

        add(own.at[r, 0:C], ext.at[r, EXT - C : EXT], below[0])
        add(own.at[r, ROWS - C : ROWS], ext.at[r, 0:C], above[0])
        for p in range(3):
            add(faces.at[r, 0], edges_in.at[r, 1, p], below[1 + p])
            add(faces.at[r, 1], edges_in.at[r, 0, p], above[1 + p])
        for p in range(3):
            add(faces.at[r], faces_in.at[r, p], flips[p])
        return copies

    def give(r, field):
        own[r] = field
        border = dot(field, sel[...])
        for v in range(2):
            faces[r, v] = pick(group, [border[128 * v + C * g : 128 * v + C * g + C] for g in range(4)]).astype(BF16)
        copies = halo_copies(r)
        for copy in copies:
            copy.start()
        ext[r, C : EXT - C] = field
        return copies

    def take(r, copies):
        for copy in copies:
            copy.wait_recv()
        none = jnp.zeros((C, 128), F32)
        for side, there, g, lo in ((0, has_below, 3, 0), (1, has_above, 0, EXT - C)):
            ext[r, lo : lo + C] = jnp.where(there, ext[r, lo : lo + C].astype(F32), 0.0).astype(BF16)
            by_y, by_z, by_yz = (edges_in[r, side, p].astype(F32) for p in range(3))
            here = there & (group == g)
            beside[lo : lo + C, :128] = jnp.where(here, jnp.where(within < 16, by_y, by_z), none).astype(BF16)
            beside[lo : lo + C, 128:] = jnp.where(here, by_yz, none).astype(BF16)
        for v in range(2):
            by_y, by_z, by_yz = (faces_in[r, p, v].astype(F32) for p in range(3))
            by_yz_ = by_yz
            both = jnp.where(within < 16, by_y, by_z)
            for g in range(4):
                lo = C * (1 + 4 * v + g)
                beside[lo : lo + C, :128] = jnp.where(group == g, both, none).astype(BF16)
                beside[lo : lo + C, 128:] = jnp.where(group == g, by_yz_, none).astype(BF16)
        halo[...] = dot(beside[...], expand[...])
        lane = iota((1, 128), 1)

        def rows_of(i, carry):
            rows = pl.ds(pl.multiple_of(i * C, C), C)
            u = [ext[r, rows, 128 * v : 128 * v + 128].astype(F32) for v in range(2)]
            for oz in (-1, 0, 1):
                if oz == 0:
                    s = u
                else:
                    edge = lane % 16 == (15 if oz == 1 else 0)
                    s = [
                        jnp.where(edge, halo[rows, 128 * v : 128 * v + 128], pltpu.roll(u[v], (-oz) % 128, 1))
                        for v in range(2)
                    ]
                beyond_y = halo[rows, 384 + 128 * oz : 512 + 128 * oz]
                up = [pltpu.roll(s[v], 112, 1) for v in range(2)]
                down = [pltpu.roll(s[v], 16, 1) for v in range(2)]
                results = (
                    (jnp.where(lane < 16, beyond_y, down[0]), jnp.where(lane < 16, down[0], down[1])),
                    s,
                    (jnp.where(lane >= 112, up[1], up[0]), jnp.where(lane >= 112, beyond_y, up[1])),
                )
                for oy in range(3):
                    at = pl.ds(pl.multiple_of((oy * 3 + oz + 1) * EXT + i * C, C), C)
                    for v in range(2):
                        shifted[r, at, 128 * v : 128 * v + 128] = results[oy][v].astype(BF16)
            return carry

        lax.fori_loop(0, 10, rows_of, 0)

    def filter_rows(f):
        for g8 in range(108):
            tap, b = g8 // 4, g8 % 4
            src, rr = g8 // 27, g8 % 27
            g, r = rr // 7, rr % 7
            ox, t = tap // 9, tap % 9
            part = wrecv[f, src, 16 * (r // 2) : 16 * (r // 2) + 16].astype(F32)[8 * (r % 2) : 8 * (r % 2) + 8]
            wrows[t * 128 + ox * C + 8 * b : t * 128 + ox * C + 8 * b + 8] = jnp.where(group == g, part, 0.0)

    def band(slot, t, value):
        lane = iota((1, 128), 1)
        for turn in (0, 32, 64, 96):
            turned = value if turn == 0 else pltpu.roll(value, turn, 1)
            for xo in range(8):
                at = t * EXT + C * xo
                if at % 128 != turn:
                    continue
                v = at // 128
                rows = slice(C * xo, C * xo + C)
                if turn <= 32:
                    banded[slot, rows, 128 * v : 128 * v + 128] = turned.astype(BF16)
                else:
                    banded[slot, rows, 128 * v : 128 * v + 128] = jnp.where(lane >= turn, turned, 0.0).astype(BF16)
                    banded[slot, rows, 128 * v + 128 : 128 * v + 256] = jnp.where(lane < turn, turned, 0.0).astype(BF16)

    def band_forward(f):
        eye = spread(iota((C, 128), 1) % C == iota((C, 128), 0))
        turned = dot(eye, wrows[...].astype(BF16), NT)
        for t in range(9):
            band(f, t, turned[:, 128 * t : 128 * t + 128])

    def band_back(f):
        lanes = iota((128, 128), 1)
        ins = iota((128, 128), 0) % C
        for t in range(9):
            value = None
            for ox in range(3):
                place = spread(lanes == C * (2 - ox) + ins)
                part = dot(wrows[t * 128 + ox * C : t * 128 + ox * C + C].astype(BF16), place)
                value = part if value is None else value + part
            band(2 + f, 8 - t, value)

    def conv(slot, r):
        return dot(banded[slot], shifted[r])

    def logistic(v):
        return 1.0 / (1.0 + jnp.exp(-v))

    def depart(slot, field, out):
        vout[slot] = dot(perm_back[...], field).reshape(C, 8, CELLS).astype(BF16)
        copy = pltpu.make_async_copy(vout.at[slot], out.at[0, 0], out_sem.at[slot])
        copy.start()
        return copy

    def filter_gradient(f, r, gradient):
        product[...] = dot(shifted[r, 0:DEPTH], gradient, NT)

        def term(g8):
            tap, b = g8 // 4, g8 % 4
            ox, t = tap // 9, tap % 9
            halves = []
            for v in range(2):
                parts = []
                for g in range(4):
                    at = t * EXT + (4 * v + g + ox) * C + 8 * b
                    parts.append(product[at : at + 8, 128 * v : 128 * v + 128])
                halves.append(pick(group, parts))
            return halves[0] + halves[1]

        odd, high = group % 2 == 1, group >= 2
        tiles = []
        for rr in range(27):
            a = [term(27 * y + rr) for y in range(4)]
            pairs = [
                jnp.where(odd, a[i + 1], a[i]) + pltpu.roll(jnp.where(odd, a[i], a[i + 1]), 32, 1) for i in (0, 2)
            ]
            tiles.append(
                jnp.where(high, pairs[1], pairs[0]) + pltpu.roll(jnp.where(high, pairs[0], pairs[1]), 64, 1)
            )
        tiles.append(jnp.zeros((8, 128), F32))
        for j in range(14):
            pile[f, j] = jnp.concatenate(tiles[2 * j : 2 * j + 2], axis=0).astype(BF16)
        for j in range(14, GROUP):
            pile[f, j] = jnp.zeros((16, 128), BF16)

    def scatter(f):
        copies = []
        for i, d in enumerate(zc_peers):
            copies.append(
                pltpu.make_async_remote_copy(
                    src_ref=pile.at[f, lax.rem(zc + i + 1, GROUP)], dst_ref=scattered.at[f, i],
                    send_sem=rs_send.at[f, i], recv_sem=rs_recv.at[f, i], device_id=(d, dp), device_id_type=MESH,
                )
            )
            copies[-1].start()
        return copies

    def collect(f, copies):
        total = pile[f, zc].astype(F32)
        for i, copy in enumerate(copies):
            copy.wait_recv()
            total = total + scattered[f, i].astype(F32)
        return total

    dp_peers = [(space, lax.rem(dp + i, 4)) for i in range(1, 4)]
    loads[0].wait()
    source = (arrive(vin) * keep).astype(BF16)

    pl.semaphore_wait(barrier, len(greeted))

    moves = []
    for f in range(2):
        row_moves = []
        for i, peer in enumerate(dp_peers):
            row_moves.append(
                pltpu.make_async_remote_copy(
                    src_ref=wsend.at[f], dst_ref=wrecv.at[f, dp], send_sem=filt_send.at[f, i],
                    recv_sem=filt_recv.at[f, i], device_id=peer, device_id_type=MESH,
                )
            )
        moves.append(row_moves)
    for move in moves[0]:
        move.start()
    sent = give(0, source)
    for move in moves[1]:
        move.start()
    halos = [sent]

    loads[1].wait()
    upstream = arrive(cin) * keep

    for move in moves[0]:
        move.wait_recv()
    filter_rows(0)
    band_forward(0)
    take(0, halos[0])
    pre_one = conv(0, 0)
    gate_one = logistic(pre_one)
    halos.append(give(1, (pre_one * gate_one * keep).astype(BF16)))
    slope_one = (gate_one + pre_one * gate_one * (1.0 - gate_one)) * keep

    band_back(0)
    for move in moves[1]:
        move.wait_recv()
    filter_rows(1)
    band_forward(1)
    take(1, halos[1])
    pre_two = conv(1, 1)
    gate_two = logistic(pre_two)
    grad_two = (upstream * (gate_two + pre_two * gate_two * (1.0 - gate_two))).astype(BF16)
    halos.append(give(2, grad_two))
    outs = [depart(0, (pre_two * gate_two * keep).astype(BF16), act_out)]
    band_back(1)
    filter_gradient(1, 1, grad_two)
    piles_two = scatter(1)
    take(2, halos[2])
    grad_one = (conv(3, 2) * slope_one).astype(BF16)
    halos.append(give(3, grad_one))
    filter_gradient(0, 0, grad_one)
    piles_one = scatter(0)
    total_two = collect(1, piles_two)
    take(3, halos[3])
    outs.append(depart(1, (conv(2, 3) * keep).astype(BF16), gin_out))
    total_one = collect(0, piles_one)

    parts = [total_one[:8], total_one[8:], total_two[:8], total_two[8:]]
    odd, high = group % 2 == 1, group >= 2
    one_up = lambda v: pltpu.roll(v, 32, 1)
    one_down = lambda v: pltpu.roll(v, 96, 1)
    half = []
    for i in (0, 2):
        half.append(
            (jnp.where(odd, one_up(parts[i + 1]), parts[i]), jnp.where(odd, parts[i + 1], one_down(parts[i])))
        )
    for i in range(2):
        lo, hi = half[0][i], half[1][i]
        summed[i] = jnp.where(high, pltpu.roll(hi, 64, 1), lo)
        summed[2 + i] = jnp.where(high, hi, pltpu.roll(lo, 64, 1))

    crossing = []
    for i, ((d, y), _) in enumerate(zip(xy_peers, xy_slots)):
        crossing.append(
            pltpu.make_async_remote_copy(
                src_ref=summed.at[y], dst_ref=crossed.at[i], send_sem=xy_send.at[i], recv_sem=xy_recv.at[i],
                device_id=(d, y), device_id_type=MESH,
            )
        )
        crossing[-1].start()
    total = summed[dp]
    for i, copy in enumerate(crossing):
        copy.wait_recv()
        total = total + crossed[i]
    total = total * (1.0 / math.sqrt(4 * count * 2048))
    final[...] = total
    gathered[zc] = total
    spreading = []
    for i, d in enumerate(zc_peers):
        spreading.append(
            pltpu.make_async_remote_copy(
                src_ref=final, dst_ref=gathered.at[zc], send_sem=ag_send.at[i], recv_sem=ag_recv.at[i],
                device_id=(d, dp), device_id_type=MESH,
            )
        )
        spreading[-1].start()
    for copy in spreading:
        copy.wait_recv()
    for j in range(14):
        value = gathered[j]
        for h in range(2):
            if j == 13 and h == 1:
                continue
            at = 16 * j + 8 * h
            lo = value if h == 0 else pltpu.roll(value, 96, 1)
            grad_one_out[at : at + 8, :] = lo[:, :C]
            grad_two_out[at : at + 8, :] = pltpu.roll(value, 64 - 32 * h, 1)[:, :C]

    for copy in outs:
        copy.wait()
    for copies in halos + moves + [piles_one, piles_two, crossing, spreading]:
        for copy in copies:
            copy.wait_send()


def on_device(volume, tissue_kept, filter_one, filter_two, cotangent):
    vmem, anywhere = pl.BlockSpec(memory_space=pltpu.VMEM), pl.BlockSpec(memory_space=pl.ANY)
    dma = pltpu.SemaphoreType.DMA
    field = jax.ShapeDtypeStruct(volume.shape, BF16)
    grad = jax.ShapeDtypeStruct(filter_one.shape, F32)
    return pl.pallas_call(
        kernel,
        out_shape=(field, field, grad, grad),
        in_specs=[pl.BlockSpec(memory_space=pltpu.SMEM), vmem, vmem, anywhere, anywhere],
        out_specs=(anywhere, anywhere, vmem, vmem),
        scratch_shapes=[
            pltpu.VMEM((C, 8, CELLS), BF16),
            pltpu.VMEM((C, 8, CELLS), BF16),
            pltpu.VMEM((2, C, 8, CELLS), BF16),
            pltpu.VMEM((4, ROWS, CELLS), BF16),
            pltpu.VMEM((4, 2, C, 128), BF16),
            pltpu.VMEM((4, 3, 2, C, 128), BF16),
            pltpu.VMEM((4, 2, 3, C, 128), BF16),
            pltpu.VMEM((4, EXT, CELLS), BF16),
            pltpu.VMEM((EXT, 256), BF16),
            pltpu.VMEM((EXT, 640), F32),
            pltpu.VMEM((4, PAD, CELLS), BF16),
            pltpu.VMEM((4, ROWS, PAD), BF16),
            pltpu.VMEM((2, 64, 128), BF16),
            pltpu.VMEM((2, 4, 64, 128), BF16),
            pltpu.VMEM((9 * 128, 128), F32),
            pltpu.VMEM((8, 128), F32),
            pltpu.VMEM((DEPTH, CELLS), F32),
            pltpu.VMEM((2, GROUP, 16, 128), BF16),
            pltpu.VMEM((2, GROUP - 1, 16, 128), BF16),
            pltpu.VMEM((4, 8, 128), F32),
            pltpu.VMEM((GROUP - 1, 8, 128), F32),
            pltpu.VMEM((8, 128), F32),
            pltpu.VMEM((GROUP, 8, 128), F32),
            pltpu.VMEM((CELLS, 128), BF16),
            pltpu.VMEM((256, 640), BF16),
            pltpu.VMEM((256, 256), BF16),
            pltpu.VMEM((256, 256), BF16),
            dma((2,)), dma((2,)), dma((4, 11)), dma((4, 11)), dma((2, 3)), dma((2, 3)),
            dma((2, GROUP - 1)), dma((2, GROUP - 1)), dma((GROUP - 1,)), dma((GROUP - 1,)),
            dma((GROUP - 1,)), dma((GROUP - 1,)),
        ],
        compiler_params=pltpu.CompilerParams(
            collective_id=0, has_side_effects=True, vmem_limit_bytes=48 * 1024 * 1024
        ),
    )(tissue_kept, filter_one, filter_two, volume, cotangent)


def solution(mesh):
    field, rows = P("dp", "space", None, None, None), P("dp", None)
    return jax.shard_map(
        on_device,
        mesh=mesh,
        in_specs=(field, P("dp", "space", None), rows, rows, field),
        out_specs=(field, field, rows, rows),
        check_vma=False,
    )
```

time: 529 us -> 65 us (0.12)
  the two profiles are of different devices: /device:TPU:2 before, /device:TPU:1 now
where the time goes in v1:
time: 65 us; the launch traced here: 64.7 us
  Pallas kernels  58.7 us (90%)
  local copies, waits for them, and re-layouts  5.3 us (8%)
  between operations  0.68 us (1%)
    pallas_call x1, Pallas kernels, on_device(): pl.pallas_call(kernel, out_shape=(field, field, grad, grad), in_specs=[pl...  58.7 us
    unnamed x10, local copies, waits for them, and re-layouts  3.92 us
    pallas_call x2, local copies, waits for them, and re-layouts, on_device(): pl.pallas_call(kernel, out_shape=(field, field, grad, grad), in_specs=[pl...  1.38 us

profile of v1, /device:TPU:1, one launch (start us, length us, event | category | flops | bytes accessed | tf_op | source)
XLA Modules:
  0.0 64.7 jit_solution(13257407607924407075)
XLA Ops:
  0.6 0.0 copy-start
  0.6 0.9 %copy.9.filter_one = bf16[216,32]{1,0:T(8,128)(2,1)S(1)} copy(bf16[216,32]{0,1:T(8,128)(2,1)} %param.7) | data formatting | bytes 27648 | tf_op args[2]
  1.5 0.0 copy-start.2
  1.5 0.8 %copy.10.filter_two = bf16[216,32]{1,0:T(8,128)(2,1)S(1)} copy(bf16[216,32]{0,1:T(8,128)(2,1)} %param.8) | data formatting | bytes 27648 | tf_op args[3]
  2.4 0.0 copy-done
  2.4 0.0 copy-done.2
  2.4 0.0 copy-start.1
  2.4 0.9 %copy-done.1 = bf16[1,1,32,8,256]{4,3,2,1,0:T(8,128)(2,1)S(1)} copy-done((bf16[1,1,32,8,256]{4,3,2,1,0:T(8,128)(2,1)S(1)}, bf16[1,1,32,8,256]{4,3,2,1,0:T(8,128)(2,1)}, u32[]{:S(2)}) %copy-start.1) | copy-done | bytes 131096
  3.3 58.7 %shard_map.84 = (bf16[1,1,32,8,256]{4,3,2,1,0:T(8,128)(2,1)S(1)}, bf16[1,1,32,8,256]{4,3,2,1,0:T(8,128)(2,1)S(1)}, f32[216,32]{1,0:T(8,128)S(1)}, f32[216,32]{1,0:T(8,128)S(1)}) custom-call(s32[1,1,4]{2,1,0:T(1,128)S(1)} %copy-done.2, bf16[216,32]{1,0:T(8,128)(2,1)S(1)} %copy.9.filter_one, bf16[216,32]{1,0:T(8,128)(2,1)S(1)} %copy.10.filter_two, ...), custom_call_target="tpu_custom_call" | custom-call | tf_op jit(solution)/shard_map/pallas_call | solution.py:441
  62.0 0.7 %copy.11 = f32[216,32]{0,1:T(8,128)} copy(f32[216,32]{1,0:T(8,128)S(1)} %get-tuple-element.6) | data formatting | bytes 55296 | tf_op jit(solution)/shard_map/pallas_call | solution.py:441
  62.7 0.7 %copy.12 = f32[216,32]{0,1:T(8,128)} copy(f32[216,32]{1,0:T(8,128)S(1)} %get-tuple-element.7) | data formatting | bytes 55296 | tf_op jit(solution)/shard_map/pallas_call | solution.py:441
  63.4 0.7 %copy.15 = bf16[1,1,32,8,256]{4,3,2,1,0:T(8,128)(2,1)} copy(bf16[1,1,32,8,256]{4,3,2,1,0:T(8,128)(2,1)S(1)} %get-tuple-element.12) | data formatting | bytes 262144
  64.1 0.7 %copy.16 = bf16[1,1,32,8,256]{4,3,2,1,0:T(8,128)(2,1)} copy(bf16[1,1,32,8,256]{4,3,2,1,0:T(8,128)(2,1)S(1)} %get-tuple-element.13) | data formatting | bytes 262144
Async XLA Ops:
  0.6 1.7 %copy-start = (bf16[1,1,32,8,256]{4,3,2,1,0:T(8,128)(2,1)S(1)}, bf16[1,1,32,8,256]{4,3,2,1,0:T(8,128)(2,1)}, u32[]{:S(2)}) copy-start(bf16[1,1,32,8,256]{4,3,2,1,0:T(8,128)(2,1)} %volume.1) | copy-start | bytes 393220
  1.5 0.9 %copy-start.2 = (s32[1,1,4]{2,1,0:T(1,128)S(1)}, s32[1,1,4]{2,1,0:T(1,128)}, u32[]{:S(2)}) copy-start(s32[1,1,4]{2,1,0:T(1,128)} %kept.1) | copy-start | bytes 52
  2.4 0.9 %copy-start.1 = (bf16[1,1,32,8,256]{4,3,2,1,0:T(8,128)(2,1)S(1)}, bf16[1,1,32,8,256]{4,3,2,1,0:T(8,128)(2,1)}, u32[]{:S(2)}) copy-start(bf16[1,1,32,8,256]{4,3,2,1,0:T(8,128)(2,1)} %cotangent.1) | copy-start | bytes 393220

commit v2 on v0

v2 whole, which is shorter than its diff:
```python
import math

import jax
import jax.numpy as jnp
from jax import lax
from jax.experimental import pallas as pl
from jax.experimental.pallas import tpu as pltpu
from jax.sharding import PartitionSpec as P

MESH = pl.DeviceIdType.MESH
F32 = jnp.float32
BF16 = jnp.bfloat16
NN = (((1,), (0,)), ((), ()))
NT = (((1,), (1,)), ((), ()))
TN = (((0,), (0,)), ((), ()))

C = 32
GONE = 64.0
STARTS = (0, 6, 13, 20)


def dot(a, b, dims=NN):
    return lax.dot_general(a, b, dims, preferred_element_type=F32)


def iota(shape, axis):
    return lax.broadcasted_iota(jnp.int32, shape, axis)


def ones_at(cond):
    return jnp.where(cond, 1.0, 0.0).astype(BF16)


def pick(group, parts):
    value = None
    for g in range(len(parts) - 1, -1, -1):
        part = 0.0 if parts[g] is None else parts[g]
        if value is None:
            value = part
        elif not (parts[g] is None and isinstance(value, float)):
            value = jnp.where(group == g, part, value)
    return value


def logistic(v):
    return 1.0 / (1.0 + jnp.exp(-v))


def tiles(count, body, unroll=3):
    def step(i, carry):
        for u in range(unroll):
            body(pl.multiple_of((i * unroll + u) * 16, 16))
        return carry

    lax.fori_loop(0, count // unroll, step, 0)
    for i in range(count // unroll * unroll, count):
        body(i * 16)


def layout(h):
    yrows = 32 if h == 3 else 16
    low, high, beyond = 128, 128 + 16 * h, 128 + 32 * h
    return yrows, low, high, beyond, beyond + yrows, beyond + yrows + 16, beyond + yrows + 32


def kernel(
    kept, filter_one, filter_two, volume, cotangent,
    act_out, gin_out, grad_one_out, grad_two_out,
    vin, cin, vout, spread, nat, nat_main, nat_z, face_main, face_z, stack_main, stack_z,
    blk, cot, keep, slope, pre, shifted, bands, leaving, owned, wide,
    wsend, wrecv, wrows, rep, product, tap_tile, pile, pair_in, crossing, xy_in, z_in, xc_in, final,
    turn, copies8, sel3, sel1, rows3, rows1, place0, place1, place2, pack, unplace, inside,
    local_sem, out_sem, halo_send, halo_recv, filt_send, filt_recv,
    pair_send, pair_recv, xy_send, xy_recv, z_send, z_recv, xc_send, xc_recv,
):
    space = lax.axis_index("space")
    dp = lax.axis_index("dp")
    count = lax.axis_size("space")
    rx, ry, rz = space // 4, (space // 2) % 2, space % 2
    bx, pz = space // 16, (space // 2) % 8
    has_below, has_above = rx > 0, rx < count // 4 - 1
    started = []

    loads = [
        pltpu.make_async_copy(volume.at[0, 0], vin, local_sem.at[0]),
        pltpu.make_async_copy(cotangent.at[0, 0], cin, local_sem.at[1]),
    ]
    for load in loads:
        load.start()

    def send(src, dst, sems, at, peer):
        copy = pltpu.make_async_remote_copy(
            src_ref=src, dst_ref=dst, send_sem=sems[0].at[at], recv_sem=sems[1].at[at],
            device_id=peer, device_id_type=MESH,
        )
        copy.start()
        started.append(copy)
        return copy

    base = space - 2 * ry - rz
    column = (space, base + 2 * (1 - ry) + rz, base + 2 * ry + (1 - rz), base + 2 * (1 - ry) + (1 - rz))
    below = [lax.rem(d - 4 + count, count) for d in column]
    above = [lax.rem(d + 4, count) for d in column]
    xy = bx * 4 + dp
    xy_slots = [lax.rem(xy + k, 16) for k in range(1, 16)]
    xy_peers = [((s // 4) * 16 + lax.rem(space, 16), s % 4) for s in xy_slots]
    z_peers = [(bx * 16 + 2 * lax.rem(pz + k, 8) + rz, dp) for k in range(1, 8)]
    xc = rz * 4 + bx
    xc_slots = [lax.rem(xc + k, 8) for k in range(1, 8)]
    xc_peers = [((s % 4) * 16 + 2 * pz + s // 4, dp) for s in xc_slots]
    dp_peers = [(space, lax.rem(dp + k, 4)) for k in range(1, 4)]

    barrier = pltpu.get_barrier_semaphore()
    greeted = [(d, dp) for d in column[1:]] + [(d, dp) for d in below + above] + xy_peers + z_peers + xc_peers
    for peer in greeted:
        pl.semaphore_signal(barrier, inc=1, device_id=peer, device_id_type=MESH)

    group = iota((1, 128), 1) // C

    row, col = iota((256, 256), 0), iota((256, 256), 1)
    y, z = row % 16, row // 16
    turn[...] = ones_at(col == 16 * jnp.where(ry == 0, y, 15 - y) + jnp.where(rz == 0, z, 15 - z))
    row, col = iota((256, 128), 0), iota((256, 128), 1)
    for x in range(8):
        copies8[:, 128 * x : 128 * x + 128] = ones_at(row == 8 * (col % C) + x)

    def faces_of(h):
        row, col = iota((32 * h, 128), 0), iota((32 * h, 128), 1)
        y, x = col // 8, col % 8
        return ones_at(
            ((x < h) & (row == h * y + x)) | ((x >= 8 - h) & (row == 16 * h + h * y + x - (8 - h)))
        )

    sel3[...] = faces_of(3)

    cell = iota((1, 256), 1)
    tile = 2 * (cell // 128) + (cell % 16) // 8
    kept_cells = jnp.zeros((1, 256), F32)
    for b in range(4):
        kept_cells = jnp.where(tile == b, kept[0, 0, b].astype(F32), kept_cells)

    def turn_in(f, field):
        cells = dot(turn[...], field.astype(BF16), NT).astype(BF16)
        spread[...] = dot(cells, copies8[...])
        for x in range(8):
            for w in range(5):
                layers = [4 * w + g for g in range(4)] if w < 4 else [None, 15, 14, 13]
                parts = [None if l is None else spread[16 * l : 16 * l + 16, 128 * x : 128 * x + 128] for l in layers]
                nat[w, pl.ds(x, 16, stride=8), :] = pick(group, parts)
        return jnp.concatenate([nat[w] for w in range(5)], axis=1).astype(BF16)

    def give(f, h, sel, field):
        yrows, low, high, beyond, corner_low, corner_high, _ = layout(h)
        main, last = field[:, :512], field[:, 512:]
        nat_main[f] = main
        nat_z[f] = last
        faces = dot(sel, field).astype(BF16)
        for side in range(2):
            face_main[f, side, 0 : 16 * h] = faces[16 * h * side : 16 * h * side + 16 * h, :512]
            face_z[f, side, 0 : 16 * h] = faces[16 * h * side : 16 * h * side + 16 * h, 512:]
        moves = []

        def add(src, dst, d):
            moves.append(send(src, dst, (halo_send, halo_recv), (f, len(moves)), (d, dp)))

        ends = ((1, low, corner_low, above), (0, high, corner_high, below))
        for side, at, _, to in ends:
            add(face_main.at[f, side, 0 : 16 * h], stack_main.at[f, at : at + 16 * h], to[0])
        for side, at, corner, to in ends:
            add(face_z.at[f, side, 0 : 16 * h], stack_z.at[f, at : at + 16 * h], to[2])
            add(face_main.at[f, side, 16 * h - 16 : 16 * h], stack_main.at[f, corner : corner + 16], to[1])
            add(face_z.at[f, side, 16 * h - 16 : 16 * h], stack_z.at[f, corner : corner + 16], to[3])
        add(nat_main.at[f, 128 - yrows : 128], stack_main.at[f, beyond : beyond + yrows], column[1])
        add(nat_z.at[f, 128 - yrows : 128], stack_z.at[f, beyond : beyond + yrows], column[3])
        add(nat_z.at[f], stack_z.at[f, 0:128], column[2])
        stack_main[f, 0:128] = main
        return moves

    def assemble(h):
        yrows, low, high, beyond, corner_low, corner_high, total = layout(h)
        row, col = iota((304, total), 0), iota((304, total), 1)
        y, x = row // 16, row % 16 - 4
        mid, lo, hi = (x >= 0) & (x < 8), (x < 0) & (x >= -h), (x >= 8) & (x < 8 + h)
        own, far = y < 16, (y >= 16) & (y < 16 + h)
        first, there = 16 - yrows // 8, 31 - y
        skip = 16 * h - 16
        at = jnp.where(own & mid, 8 * y + x, -1)
        at = jnp.where(own & lo, low + h * y + x + h, at)
        at = jnp.where(own & hi, high + h * y + x - 8, at)
        at = jnp.where(far & mid, beyond + 8 * (there - first) + x, at)
        at = jnp.where(far & lo, corner_low + h * there + x + h - skip, at)
        at = jnp.where(far & hi, corner_high + h * there + x - 8 - skip, at)
        return ones_at(at == col)

    def take(f, h, rows, moves):
        for move in moves:
            move.wait_recv()
        total = layout(h)[-1]
        pieces = jnp.concatenate([stack_main[f, 0:total], stack_z[f, 0:total]], axis=1)
        whole = dot(rows, pieces).astype(BF16)
        return (
            dot(whole[:, 0:256], place0[...]), dot(whole[:, 128:512], place1[...]), dot(whole[:, 256:640], place2[...])
        )

    def put(f, b, v, r0, value):
        lanes = slice(128 * v, 128 * v + 128)
        at = pl.ds(r0 + 16, 16)
        shifted[f, 1, b, at, lanes] = value.astype(BF16)
        shifted[f, 0, b, at, lanes] = pltpu.roll(value, 1, 0).astype(BF16)
        shifted[f, 2, b, at, lanes] = pltpu.roll(value, 15, 0).astype(BF16)

    def put_all(f, r0, parts):
        for b in range(3):
            lo, hi = parts[b]
            lo = jnp.where(group == 0, pltpu.roll(parts[b - 1][1], 64, 1) if b > 0 else 0.0, lo)
            hi = jnp.where(group == 3, pltpu.roll(parts[b + 1][0], 64, 1) if b < 2 else 0.0, hi)
            put(f, b, 0, r0, lo)
            put(f, b, 1, r0, hi)

    def inputs_of(f, ox, oy, ny):
        return shifted[f, ox, :, 16 * oy : 16 * oy + 16 * ny].reshape(48 * ny, 256)

    def conv(f, slot, ny, back):
        lhs = jnp.concatenate([inputs_of(f, ox, oy, ny) for ox in range(3) for oy in range(3)], axis=1)
        if back:
            rhs, dims = jnp.concatenate([bands[slot, t] for t in range(9)], axis=1), NT
        else:
            rhs, dims = bands[slot].reshape(9 * 256, 256), NN
        pre[:, 0 : 16 * ny] = dot(lhs, rhs, dims).reshape(3, 16 * ny, 256)

    def send_rows(f, rows):
        square = ones_at(iota((216, 216), 0) == iota((216, 216), 1))
        four = jnp.concatenate([rows[...]] * 4, axis=0)
        full = jnp.concatenate([dot(square, four, NT), jnp.zeros((8, 128), F32)], axis=0)
        packed = pick(group, [full[56 * g : 56 * g + 56] for g in range(4)])
        packed = jnp.concatenate([packed, jnp.zeros((8, 128), F32)], axis=0).astype(BF16)
        wsend[f] = packed
        wrecv[f, dp] = packed

    def share_rows(f):
        return [
            send(wsend.at[f], wrecv.at[f, dp], (filt_send, filt_recv), (f, i), peer) for i, peer in enumerate(dp_peers)
        ]

    def filter_rows(f):
        for g8 in range(108):
            src, rr = g8 // 27, g8 % 27
            g, r = rr // 7, rr % 7
            part = wrecv[f, src, 16 * (r // 2) : 16 * (r // 2) + 16].astype(F32)[8 * (r % 2) : 8 * (r % 2) + 8]
            wrows[8 * g8 : 8 * g8 + 8] = jnp.where(group == g, part, 0.0)
        again = ones_at(iota((128, 128), 0) % C == iota((128, 128), 1) % C)
        rep[f] = dot(wrows[...].astype(BF16), again).reshape(27, C, 128)

    def tap(ox, oy, oz):
        ty = oy if oy == 1 else jnp.where(ry == 0, oy, 2 - oy)
        tz = oz if oz == 1 else jnp.where(rz == 0, oz, 2 - oz)
        return 9 * ox + 3 * ty + tz

    def band(f):
        for ox in range(3):
            for oy in range(3):
                taps = [rep[f, tap(ox, oy, oz)] for oz in range(3)]
                for v in range(2):
                    for zi in range(8):
                        parts = []
                        for g in range(4):
                            zo = 4 * v + g
                            parts.append(taps[zi - zo + 1] if 1 <= zo <= 6 and abs(zi - zo) <= 1 else None)
                        if any(p is not None for p in parts):
                            value = pick(group, parts).astype(BF16)
                        else:
                            value = jnp.zeros((C, 128), BF16)
                        bands[f, 3 * ox + oy, C * zi : C * zi + C, 128 * v : 128 * v + 128] = value

    def band_back(f):
        for sx in range(3):
            for sy in range(3):
                taps = [rep[f, tap(2 - sx, 2 - sy, oz)] for oz in range(3)]
                for v in range(2):
                    for zo in range(8):
                        parts = []
                        for g in range(4):
                            zi = 4 * v + g
                            parts.append(taps[zo - zi + 1] if 1 <= zo <= 6 and abs(zi - zo) <= 1 else None)
                        if any(p is not None for p in parts):
                            value = pick(group, parts).astype(BF16)
                        else:
                            value = jnp.zeros((C, 128), BF16)
                        bands[2 + f, 3 * sx + sy, C * zo : C * zo + C, 128 * v : 128 * v + 128] = value

    def natural(blocked):
        rows = jnp.concatenate([dot(pack[...], blocked[b]) for b in range(3)], axis=1).astype(BF16)
        return dot(rows, unplace[...])

    def depart(slot, field, out):
        for w in range(4):
            nat[w] = field[:, 128 * w : 128 * w + 128]
        for x in range(8):
            for w in range(4):
                value = nat[w, pl.ds(x, 16, stride=8), :]
                for g in range(4):
                    at = 16 * (4 * w + g)
                    wide[at : at + 16, 128 * x : 128 * x + 128] = jnp.where(group == g, value, 0.0).astype(BF16)
        cells = dot(copies8[...], wide[...], NT).astype(BF16)
        vout[slot] = dot(cells, turn[...]).reshape(C, 8, 256).astype(BF16)
        copy = pltpu.make_async_copy(vout.at[slot], out.at[0, 0], out_sem.at[slot])
        copy.start()
        return copy

    def filter_gradient(f, r):
        gradient = owned[f].reshape(768, 256)
        odd, high = group % 2 == 1, group >= 2
        for t in range(9):
            product[t] = dot(gradient, inputs_of(r, t // 3, t % 3, 16), TN)
        for t in range(9):
            for oz in range(3):
                a = []
                for j in range(4):
                    halves = []
                    for v in range(2):
                        parts = []
                        for g in range(4):
                            zo = 4 * v + g - (oz - 1)
                            at = zo * C + 8 * j
                            parts.append(product[t, at : at + 8, 128 * v : 128 * v + 128] if 1 <= zo <= 6 else None)
                        halves.append(pick(group, parts))
                    a.append(halves[0] + halves[1])
                pairs = [
                    jnp.where(odd, a[i + 1], a[i]) + pltpu.roll(jnp.where(odd, a[i], a[i + 1]), 32, 1) for i in (0, 2)
                ]
                tap_tile[f, tap(t // 3, t % 3, oz)] = jnp.where(high, pairs[1], pairs[0]) + pltpu.roll(
                    jnp.where(high, pairs[0], pairs[1]), 64, 1
                )
        for q in range(4):
            for k in range(8):
                source = STARTS[q] + k
                pile[f, k // 4, 4 * (k % 4) + q] = (
                    tap_tile[f, source] if source < 27 else jnp.zeros((8, 128), F32)
                )
        return send(pile.at[f, 1 - rz], pair_in.at[f], (pair_send, pair_recv), f, (column[2], dp))

    loads[0].wait()
    field = jnp.where(kept_cells > 0.5, vin[...].astype(F32).reshape(256, 256), GONE)
    field = turn_in(0, field)
    pl.semaphore_wait(barrier, len(greeted))
    volume_moves = give(0, 3, sel3[...], field)

    send_rows(0, filter_one)
    row_moves = [share_rows(0)]
    send_rows(1, filter_two)
    row_moves.append(share_rows(1))

    sel1[...] = faces_of(1)
    loads[1].wait()
    cot_moves = give(1, 1, sel1[...], turn_in(1, cin[...].astype(F32).reshape(256, 256)))

    rows3[...] = assemble(3)
    rows1[...] = assemble(1)
    k, n = iota((256, 256), 0), iota((256, 256), 1)
    place0[...] = ones_at(n - k == C)
    k, n = iota((384, 256), 0), iota((384, 256), 1)
    place1[...] = ones_at(k - n == C)
    place2[...] = ones_at(k - n == jnp.where(n < 160, 96, 128))
    row, col = iota((128, 256), 0), iota((128, 256), 1)
    pack[...] = ones_at(col == 16 * (row // 8) + row % 8 + 4)
    for b in range(3):
        k, n = iota((256, 640), 0), iota((256, 640), 1)
        zi, z = k // C, 6 * b + k // C - 1
        good = (zi >= 1) & (zi <= 6) & (z < 16) & (k % C == n % C)
        unplace[256 * b : 256 * b + 256] = ones_at(
            good & (((n < 512) & (n // C == z)) | ((n >= 544) & (16 - (n // C - 16) == z)))
        )
    x = iota((304, 128), 0) % 16 - 4
    inside[...] = jnp.where(((x < 0) & ~has_below) | ((x >= 8) & ~has_above), 0.0, 1.0)
    for f in range(4):
        for ox in range(3):
            for b in range(3):
                shifted[f, ox, b, 0:16] = jnp.zeros((16, 256), BF16)

    for f in range(2):
        for move in row_moves[f]:
            move.wait_recv()
        filter_rows(f)
        band(f)
        band_back(f)

    for b, value in enumerate(take(0, 3, rows3[...], volume_moves)):
        blk[b] = value

    def first(r0):
        rows = pl.ds(r0, 16)
        here = inside[rows, :]
        for b in range(3):
            for v in range(2):
                lanes = slice(128 * v, 128 * v + 128)
                value = blk[b, rows, lanes]
                kept_here = jnp.where(value == GONE, 0.0, here)
                keep[b, rows, lanes] = kept_here
                put(0, b, v, r0, value * kept_here)

    tiles(19, first)
    conv(0, 0, 18, False)

    def second(r0):
        rows = pl.ds(r0, 16)
        parts = []
        for b in range(3):
            parts.append([])
            for v in range(2):
                lanes = slice(128 * v, 128 * v + 128)
                value, there = pre[b, rows, lanes], keep[b, rows, lanes]
                gate = logistic(value)
                slope[b, rows, lanes] = (gate + value * gate * (1.0 - gate)) * there
                parts[b].append(value * gate * there)
        put_all(1, r0, parts)

    tiles(18, second)
    conv(1, 1, 17, False)
    for b, value in enumerate(take(1, 1, rows1[...], cot_moves)):
        cot[b] = value
    x = iota((16, 128), 0) - 4
    own = [jnp.where((x >= 0) & (x < 8), 1.0, 0.0)]
    own.append(jnp.where(group == 0, own[0], 0.0))

    def third(r0, last=False):
        rows = pl.ds(r0, 16)
        parts = []
        for b in range(3):
            parts.append([])
            for v in range(2):
                lanes = slice(128 * v, 128 * v + 128)
                value, there = pre[b, rows, lanes], keep[b, rows, lanes]
                gate = logistic(value)
                grad = cot[b, rows, lanes] * there * (gate + value * gate * (1.0 - gate))
                parts[b].append(grad)
                if not last:
                    leaving[b, rows, lanes] = (value * gate * there).astype(BF16)
                    owned[1, b, rows, lanes] = (grad * own[b * v // 2]).astype(BF16)
        put_all(2, r0, parts)

    tiles(16, third, 2)
    third(256, True)
    conv(2, 3, 16, True)

    def fourth(r0):
        rows = pl.ds(r0, 16)
        for b in range(3):
            for v in range(2):
                lanes = slice(128 * v, 128 * v + 128)
                grad = pre[b, rows, lanes] * slope[b, rows, lanes]
                owned[0, b, rows, lanes] = (grad * own[b * v // 2]).astype(BF16)

    tiles(16, fourth, 2)
    pair_two = filter_gradient(1, 1)
    pair_one = filter_gradient(0, 0)
    grad_moves = give(2, 1, sel1[...], natural(owned[0]).astype(BF16))
    for f, move in ((1, pair_two), (0, pair_one)):
        move.wait_recv()
        for s in range(16):
            crossing[s, f] = pile[f, rz, s] + pair_in[f, s]
    xy_moves = [
        send(crossing.at[s], xy_in.at[xy], (xy_send, xy_recv), i, peer)
        for i, (s, peer) in enumerate(zip(xy_slots, xy_peers))
    ]
    xy_in[xy] = crossing[xy]

    outs = [depart(0, natural(leaving[...]), act_out)]
    for move in xy_moves:
        move.wait_recv()
    total = xy_in[0]
    for s in range(1, 16):
        total = total + xy_in[s]
    z_in[pz] = total
    z_moves = [
        send(z_in.at[pz], z_in.at[pz], (z_send, z_recv), i, peer) for i, peer in enumerate(z_peers)
    ]

    for b, value in enumerate(take(2, 1, rows1[...], grad_moves)):
        blk[b] = value

    def fifth(r0):
        rows = pl.ds(r0, 16)
        here = inside[rows, :]
        for b in range(3):
            for v in range(2):
                put(3, b, v, r0, blk[b, rows, 128 * v : 128 * v + 128] * here)

    tiles(17, fifth, 2)
    conv(3, 2, 16, True)

    def sixth(r0):
        rows = pl.ds(r0, 16)
        for b in range(3):
            leaving[b, rows, :] = (pre[b, rows, :] * keep[b, rows, :]).astype(BF16)

    tiles(16, sixth, 2)
    outs.append(depart(1, natural(leaving[...]), gin_out))

    for move in z_moves:
        move.wait_recv()
    total = z_in[0]
    for s in range(1, 8):
        total = total + z_in[s]
    xc_in[xc] = total * (1.0 / math.sqrt(4 * count * 2048))
    xc_moves = [
        send(xc_in.at[xc], xc_in.at[xc], (xc_send, xc_recv), i, peer) for i, peer in enumerate(xc_peers)
    ]
    for move in xc_moves:
        move.wait_recv()
    offset = lax.rem(4 - dp, 4) * 8
    for f, out in enumerate((grad_one_out, grad_two_out)):
        for j in range(4):
            for w in range(2):
                parts = []
                for g in range(4):
                    value = xc_in[4 * w + g, f]
                    parts.append(value if g == j else pltpu.roll(value, 32 * ((g - j) % 4), 1))
                final[8 * j : 8 * j + 8, 128 * w : 128 * w + 128] = pick(group, parts)
        out[...] = pltpu.roll(final[...], 256 - offset, 1)[:, :216]

    for copy in outs:
        copy.wait()
    for copy in started:
        copy.wait_send()


def on_device(volume, tissue_kept, filter_one, filter_two, cotangent):
    vmem, anywhere = pl.BlockSpec(memory_space=pltpu.VMEM), pl.BlockSpec(memory_space=pl.ANY)
    dma = pltpu.SemaphoreType.DMA
    field = jax.ShapeDtypeStruct(volume.shape, BF16)
    grad = jax.ShapeDtypeStruct((C, 216), F32)
    blocked = pltpu.VMEM((3, 304, 256), F32)
    act, gin, one, two = pl.pallas_call(
        kernel,
        out_shape=(field, field, grad, grad),
        in_specs=[pl.BlockSpec(memory_space=pltpu.SMEM), vmem, vmem, anywhere, anywhere],
        out_specs=(anywhere, anywhere, vmem, vmem),
        scratch_shapes=[
            pltpu.VMEM((C, 8, 256), BF16),
            pltpu.VMEM((C, 8, 256), BF16),
            pltpu.VMEM((2, C, 8, 256), BF16),
            pltpu.VMEM((256, 1024), F32),
            pltpu.VMEM((5, 128, 128), F32),
            pltpu.VMEM((3, 128, 512), BF16),
            pltpu.VMEM((3, 128, 128), BF16),
            pltpu.VMEM((3, 2, 48, 512), BF16),
            pltpu.VMEM((3, 2, 48, 128), BF16),
            pltpu.VMEM((3, 288, 512), BF16),
            pltpu.VMEM((3, 288, 128), BF16),
            blocked,
            blocked,
            blocked,
            blocked,
            blocked,
            pltpu.VMEM((4, 3, 3, 320, 256), BF16),
            pltpu.VMEM((4, 9, 256, 256), BF16),
            pltpu.VMEM((3, 256, 256), BF16),
            pltpu.VMEM((2, 3, 256, 256), BF16),
            pltpu.VMEM((256, 1024), BF16),
            pltpu.VMEM((2, 64, 128), BF16),
            pltpu.VMEM((2, 4, 64, 128), BF16),
            pltpu.VMEM((864, 128), F32),
            pltpu.VMEM((2, 27, C, 128), F32),
            pltpu.VMEM((9, 256, 256), F32),
            pltpu.VMEM((2, 27, 8, 128), F32),
            pltpu.VMEM((2, 2, 16, 8, 128), F32),
            pltpu.VMEM((2, 16, 8, 128), F32),
            pltpu.VMEM((16, 2, 8, 128), F32),
            pltpu.VMEM((16, 2, 8, 128), F32),
            pltpu.VMEM((8, 2, 8, 128), F32),
            pltpu.VMEM((8, 2, 8, 128), F32),
            pltpu.VMEM((C, 256), F32),
            pltpu.VMEM((256, 256), BF16),
            pltpu.VMEM((256, 1024), BF16),
            pltpu.VMEM((96, 128), BF16),
            pltpu.VMEM((32, 128), BF16),
            pltpu.VMEM((304, 288), BF16),
            pltpu.VMEM((304, 208), BF16),
            pltpu.VMEM((256, 256), BF16),
            pltpu.VMEM((384, 256), BF16),
            pltpu.VMEM((384, 256), BF16),
            pltpu.VMEM((128, 256), BF16),
            pltpu.VMEM((768, 640), BF16),
            pltpu.VMEM((304, 128), F32),
            dma((2,)), dma((2,)), dma((3, 11)), dma((3, 11)), dma((2, 3)), dma((2, 3)),
            dma((2,)), dma((2,)), dma((15,)), dma((15,)), dma((7,)), dma((7,)), dma((7,)), dma((7,)),
        ],
        compiler_params=pltpu.CompilerParams(
            collective_id=0, has_side_effects=True, vmem_limit_bytes=48 * 1024 * 1024
        ),
    )(tissue_kept, filter_one.T, filter_two.T, volume, cotangent)
    return act, gin, one.T, two.T


def solution(mesh):
    field, rows = P("dp", "space", None, None, None), P("dp", None)
    return jax.shard_map(
        on_device,
        mesh=mesh,
        in_specs=(field, P("dp", "space", None), rows, rows, field),
        out_specs=(field, field, rows, rows),
        check_vma=False,
    )
```

time: 529 us -> 56.5 us (0.11)
  the two profiles are of different devices: /device:TPU:2 before, /device:TPU:1 now
where the time goes in v2:
time: 56.5 us; the launch traced here: 56.2 us
  Pallas kernels  49.1 us (87%)
  local copies, waits for them, and re-layouts  6.43 us (11%)
  between operations  0.65 us (1%)
    pallas_call x1, Pallas kernels, on_device(): pl.pallas_call(kernel, out_shape=(field, field, grad, grad), in_specs=[pl...  49.1 us
    unnamed x14, local copies, waits for them, and re-layouts  6.43 us

profile of v2, /device:TPU:1, one launch (start us, length us, event | category | flops | bytes accessed | tf_op | source)
XLA Modules:
  0.0 56.2 jit_solution(13539991902110481198)
XLA Ops:
  0.6 0.0 copy-start.4
  0.6 0.6 %copy-done.4 = s32[1,1,4]{2,1,0:T(1,128)S(1)} copy-done((s32[1,1,4]{2,1,0:T(1,128)S(1)}, s32[1,1,4]{2,1,0:T(1,128)}, u32[]{:S(2)}) %copy-start.4) | copy-done | bytes 40
  1.3 0.0 copy-start
  1.3 0.9 %copy-done = bf16[1,1,32,8,256]{4,3,2,1,0:T(8,128)(2,1)S(1)} copy-done((bf16[1,1,32,8,256]{4,3,2,1,0:T(8,128)(2,1)S(1)}, bf16[1,1,32,8,256]{4,3,2,1,0:T(8,128)(2,1)}, u32[]{:S(2)}) %copy-start) | copy-done | bytes 131096
  2.2 0.0 copy-start.1
  2.2 0.9 %copy-done.1 = bf16[1,1,32,8,256]{4,3,2,1,0:T(8,128)(2,1)S(1)} copy-done((bf16[1,1,32,8,256]{4,3,2,1,0:T(8,128)(2,1)S(1)}, bf16[1,1,32,8,256]{4,3,2,1,0:T(8,128)(2,1)}, u32[]{:S(2)}) %copy-start.1) | copy-done | bytes 131096
  3.1 0.0 copy-start.2
  3.1 0.7 %copy-done.2 = bf16[216,32]{0,1:T(8,128)(2,1)S(1)} copy-done((bf16[216,32]{0,1:T(8,128)(2,1)S(1)}, bf16[216,32]{0,1:T(8,128)(2,1)}, u32[]{:S(2)}) %copy-start.2) | copy-done | bytes 13848
  3.8 0.0 copy-start.3
  3.8 0.7 %copy-done.3 = bf16[216,32]{0,1:T(8,128)(2,1)S(1)} copy-done((bf16[216,32]{0,1:T(8,128)(2,1)S(1)}, bf16[216,32]{0,1:T(8,128)(2,1)}, u32[]{:S(2)}) %copy-start.3) | copy-done | bytes 13848
  4.5 49.1 %shard_map.84 = (bf16[1,1,32,8,256]{4,3,2,1,0:T(8,128)(2,1)S(1)}, bf16[1,1,32,8,256]{4,3,2,1,0:T(8,128)(2,1)S(1)}, f32[32,216]{1,0:T(8,128)S(1)}, f32[32,216]{1,0:T(8,128)S(1)}) custom-call(s32[1,1,4]{2,1,0:T(1,128)S(1)} %copy-done.4, bf16[32,216]{1,0:T(8,128)(2,1)S(1)} %bitcast.6, bf16[32,216]{1,0:T(8,128)(2,1)S(1)} %bitcast.7, ...), custom_call_target="tpu_custom_call" | custom-call | tf_op jit(solution)/shard_map/pallas_call | solution.py:533
  53.7 0.7 %copy.13 = bf16[1,1,32,8,256]{4,3,2,1,0:T(8,128)(2,1)} copy(bf16[1,1,32,8,256]{4,3,2,1,0:T(8,128)(2,1)S(1)} %get-tuple-element.16) | data formatting | bytes 262144
  54.3 0.7 %copy.14 = bf16[1,1,32,8,256]{4,3,2,1,0:T(8,128)(2,1)} copy(bf16[1,1,32,8,256]{4,3,2,1,0:T(8,128)(2,1)S(1)} %get-tuple-element.17) | data formatting | bytes 262144
  55.0 0.6 %copy.15 = f32[216,32]{0,1:T(8,128)} copy(f32[216,32]{0,1:T(8,128)S(1)} %bitcast.5) | data formatting | bytes 55296
  55.6 0.6 %copy.16 = f32[216,32]{0,1:T(8,128)} copy(f32[216,32]{0,1:T(8,128)S(1)} %bitcast.4) | data formatting | bytes 55296
Async XLA Ops:
  0.6 0.7 %copy-start.4 = (s32[1,1,4]{2,1,0:T(1,128)S(1)}, s32[1,1,4]{2,1,0:T(1,128)}, u32[]{:S(2)}) copy-start(s32[1,1,4]{2,1,0:T(1,128)} %kept.1) | copy-start | bytes 52
  1.3 0.9 %copy-start = (bf16[1,1,32,8,256]{4,3,2,1,0:T(8,128)(2,1)S(1)}, bf16[1,1,32,8,256]{4,3,2,1,0:T(8,128)(2,1)}, u32[]{:S(2)}) copy-start(bf16[1,1,32,8,256]{4,3,2,1,0:T(8,128)(2,1)} %volume.1) | copy-start | bytes 393220
  2.2 0.9 %copy-start.1 = (bf16[1,1,32,8,256]{4,3,2,1,0:T(8,128)(2,1)S(1)}, bf16[1,1,32,8,256]{4,3,2,1,0:T(8,128)(2,1)}, u32[]{:S(2)}) copy-start(bf16[1,1,32,8,256]{4,3,2,1,0:T(8,128)(2,1)} %cotangent.1) | copy-start | bytes 393220
  3.1 0.7 %copy-start.2 = (bf16[216,32]{0,1:T(8,128)(2,1)S(1)}, bf16[216,32]{0,1:T(8,128)(2,1)}, u32[]{:S(2)}) copy-start(bf16[216,32]{0,1:T(8,128)(2,1)} %param.7) | copy-start | bytes 41476
  3.8 0.7 %copy-start.3 = (bf16[216,32]{0,1:T(8,128)(2,1)S(1)}, bf16[216,32]{0,1:T(8,128)(2,1)}, u32[]{:S(2)}) copy-start(bf16[216,32]{0,1:T(8,128)(2,1)} %param.8) | copy-start | bytes 41476

commit v3 on v2

--- a/solution.py
+++ b/solution.py
@@ -46,17 +46,6 @@
     return 1.0 / (1.0 + jnp.exp(-v))
 
 
-def tiles(count, body, unroll=3):
-    def step(i, carry):
-        for u in range(unroll):
-            body(pl.multiple_of((i * unroll + u) * 16, 16))
-        return carry
-
-    lax.fori_loop(0, count // unroll, step, 0)
-    for i in range(count // unroll * unroll, count):
-        body(i * 16)
-
-
 def layout(h):
     yrows = 32 if h == 3 else 16
     low, high, beyond = 128, 128 + 16 * h, 128 + 32 * h
@@ -64,13 +53,13 @@
 
 
 def kernel(
-    kept, filter_one, filter_two, volume, cotangent,
+    flags, filter_one, filter_two, volume, cotangent,
     act_out, gin_out, grad_one_out, grad_two_out,
-    vin, cin, vout, spread, nat, nat_main, nat_z, face_main, face_z, stack_main, stack_z,
+    kept, rows_in, vin, cin, spread, nat, nat_main, nat_z, face_main, face_z, stack_main, stack_z,
     blk, cot, keep, slope, pre, shifted, bands, leaving, owned, wide,
     wsend, wrecv, wrows, rep, product, tap_tile, pile, pair_in, crossing, xy_in, z_in, xc_in, final,
     turn, copies8, sel3, sel1, rows3, rows1, place0, place1, place2, pack, unplace, inside,
-    local_sem, out_sem, halo_send, halo_recv, filt_send, filt_recv,
+    local_sem, halo_send, halo_recv, filt_send, filt_recv,
     pair_send, pair_recv, xy_send, xy_recv, z_send, z_recv, xc_send, xc_recv,
 ):
     space = lax.axis_index("space")
@@ -83,17 +72,25 @@
 
     loads = [
         pltpu.make_async_copy(volume.at[0, 0], vin, local_sem.at[0]),
-        pltpu.make_async_copy(cotangent.at[0, 0], cin, local_sem.at[1]),
+        pltpu.make_async_copy(flags.at[0], kept, local_sem.at[1]),
+        pltpu.make_async_copy(filter_one, rows_in.at[0], local_sem.at[2]),
+        pltpu.make_async_copy(filter_two, rows_in.at[1], local_sem.at[3]),
+        pltpu.make_async_copy(cotangent.at[0, 0], cin, local_sem.at[4]),
     ]
     for load in loads:
         load.start()
 
     def send(src, dst, sems, at, peer):
-        copy = pltpu.make_async_remote_copy(
+        pltpu.make_async_remote_copy(
             src_ref=src, dst_ref=dst, send_sem=sems[0].at[at], recv_sem=sems[1].at[at],
             device_id=peer, device_id_type=MESH,
+        ).start()
+
+    def batch(ref, sems, at):
+        copy = pltpu.make_async_remote_copy(
+            src_ref=ref, dst_ref=ref, send_sem=sems[0].at[at], recv_sem=sems[1].at[at],
+            device_id=dp_peers[0], device_id_type=MESH,
         )
-        copy.start()
         started.append(copy)
         return copy
 
@@ -135,9 +132,6 @@
 
     cell = iota((1, 256), 1)
     tile = 2 * (cell // 128) + (cell % 16) // 8
-    kept_cells = jnp.zeros((1, 256), F32)
-    for b in range(4):
-        kept_cells = jnp.where(tile == b, kept[0, 0, b].astype(F32), kept_cells)
 
     def turn_in(f, field):
         cells = dot(turn[...], field.astype(BF16), NT).astype(BF16)
@@ -150,7 +144,7 @@
         return jnp.concatenate([nat[w] for w in range(5)], axis=1).astype(BF16)
 
     def give(f, h, sel, field):
-        yrows, low, high, beyond, corner_low, corner_high, _ = layout(h)
+        yrows, low, high, beyond, corner_low, corner_high, total = layout(h)
         main, last = field[:, :512], field[:, 512:]
         nat_main[f] = main
         nat_z[f] = last
@@ -158,23 +152,23 @@
         for side in range(2):
             face_main[f, side, 0 : 16 * h] = faces[16 * h * side : 16 * h * side + 16 * h, :512]
             face_z[f, side, 0 : 16 * h] = faces[16 * h * side : 16 * h * side + 16 * h, 512:]
-        moves = []
-
-        def add(src, dst, d):
-            moves.append(send(src, dst, (halo_send, halo_recv), (f, len(moves)), (d, dp)))
+        sems = (halo_send, halo_recv)
+
+        def add(src, dst, d, kind):
+            send(src, dst, sems, (f, kind), (d, dp))
 
         ends = ((1, low, corner_low, above), (0, high, corner_high, below))
         for side, at, _, to in ends:
-            add(face_main.at[f, side, 0 : 16 * h], stack_main.at[f, at : at + 16 * h], to[0])
+            add(face_main.at[f, side, 0 : 16 * h], stack_main.at[f, at : at + 16 * h], to[0], 0)
         for side, at, corner, to in ends:
-            add(face_z.at[f, side, 0 : 16 * h], stack_z.at[f, at : at + 16 * h], to[2])
-            add(face_main.at[f, side, 16 * h - 16 : 16 * h], stack_main.at[f, corner : corner + 16], to[1])
-            add(face_z.at[f, side, 16 * h - 16 : 16 * h], stack_z.at[f, corner : corner + 16], to[3])
-        add(nat_main.at[f, 128 - yrows : 128], stack_main.at[f, beyond : beyond + yrows], column[1])
-        add(nat_z.at[f, 128 - yrows : 128], stack_z.at[f, beyond : beyond + yrows], column[3])
-        add(nat_z.at[f], stack_z.at[f, 0:128], column[2])
+            add(face_z.at[f, side, 0 : 16 * h], stack_z.at[f, at : at + 16 * h], to[2], 1)
+            add(face_main.at[f, side, 16 * h - 16 : 16 * h], stack_main.at[f, corner : corner + 16], to[1], 0)
+            add(face_z.at[f, side, 16 * h - 16 : 16 * h], stack_z.at[f, corner : corner + 16], to[3], 1)
+        add(nat_main.at[f, 128 - yrows : 128], stack_main.at[f, beyond : beyond + yrows], column[1], 0)
+        add(nat_z.at[f, 128 - yrows : 128], stack_z.at[f, beyond : beyond + yrows], column[3], 1)
+        add(nat_z.at[f], stack_z.at[f, 0:128], column[2], 1)
         stack_main[f, 0:128] = main
-        return moves
+        return [batch(stack_main.at[f, 128:total], sems, (f, 0)), batch(stack_z.at[f, 0:total], sems, (f, 1))]
 
     def assemble(h):
         yrows, low, high, beyond, corner_low, corner_high, total = layout(h)
@@ -202,9 +196,12 @@
             dot(whole[:, 0:256], place0[...]), dot(whole[:, 128:512], place1[...]), dot(whole[:, 256:640], place2[...])
         )
 
+    def halves(value):
+        return value[:, :128], value[:, 128:]
+
     def put(f, b, v, r0, value):
         lanes = slice(128 * v, 128 * v + 128)
-        at = pl.ds(r0 + 16, 16)
+        at = slice(r0 + 16, r0 + 32)
         shifted[f, 1, b, at, lanes] = value.astype(BF16)
         shifted[f, 0, b, at, lanes] = pltpu.roll(value, 1, 0).astype(BF16)
         shifted[f, 2, b, at, lanes] = pltpu.roll(value, 15, 0).astype(BF16)
@@ -220,13 +217,13 @@
     def inputs_of(f, ox, oy, ny):
         return shifted[f, ox, :, 16 * oy : 16 * oy + 16 * ny].reshape(48 * ny, 256)
 
-    def conv(f, slot, ny, back):
-        lhs = jnp.concatenate([inputs_of(f, ox, oy, ny) for ox in range(3) for oy in range(3)], axis=1)
+    def conv(f, slot, back, y0, ny):
+        lhs = jnp.concatenate([inputs_of(f, ox, y0 + oy, ny) for ox in range(3) for oy in range(3)], axis=1)
         if back:
             rhs, dims = jnp.concatenate([bands[slot, t] for t in range(9)], axis=1), NT
         else:
             rhs, dims = bands[slot].reshape(9 * 256, 256), NN
-        pre[:, 0 : 16 * ny] = dot(lhs, rhs, dims).reshape(3, 16 * ny, 256)
+        pre[slot, :, 16 * y0 : 16 * y0 + 16 * ny] = dot(lhs, rhs, dims).reshape(3, 16 * ny, 256)
 
     def send_rows(f, rows):
         square = ones_at(iota((216, 216), 0) == iota((216, 216), 1))
@@ -238,9 +235,10 @@
         wrecv[f, dp] = packed
 
     def share_rows(f):
-        return [
-            send(wsend.at[f], wrecv.at[f, dp], (filt_send, filt_recv), (f, i), peer) for i, peer in enumerate(dp_peers)
-        ]
+        sems = (filt_send, filt_recv)
+        for peer in dp_peers:
+            send(wsend.at[f], wrecv.at[f, dp], sems, f, peer)
+        return [batch(wrecv.at[f, 0:3], sems, f)]
 
     def filter_rows(f):
         for g8 in range(108):
@@ -292,7 +290,7 @@
         rows = jnp.concatenate([dot(pack[...], blocked[b]) for b in range(3)], axis=1).astype(BF16)
         return dot(rows, unplace[...])
 
-    def depart(slot, field, out):
+    def depart(field, out):
         for w in range(4):
             nat[w] = field[:, 128 * w : 128 * w + 128]
         for x in range(8):
@@ -302,29 +300,25 @@
                     at = 16 * (4 * w + g)
                     wide[at : at + 16, 128 * x : 128 * x + 128] = jnp.where(group == g, value, 0.0).astype(BF16)
         cells = dot(copies8[...], wide[...], NT).astype(BF16)
-        vout[slot] = dot(cells, turn[...]).reshape(C, 8, 256).astype(BF16)
-        copy = pltpu.make_async_copy(vout.at[slot], out.at[0, 0], out_sem.at[slot])
-        copy.start()
-        return copy
+        out[0, 0] = dot(cells, turn[...]).reshape(C, 8, 256).astype(BF16)
 
     def filter_gradient(f, r):
         gradient = owned[f].reshape(768, 256)
         odd, high = group % 2 == 1, group >= 2
         for t in range(9):
-            product[t] = dot(gradient, inputs_of(r, t // 3, t % 3, 16), TN)
-        for t in range(9):
+            product[f, t] = dot(gradient, inputs_of(r, t // 3, t % 3, 16), TN)
             for oz in range(3):
                 a = []
                 for j in range(4):
-                    halves = []
+                    sides = []
                     for v in range(2):
                         parts = []
                         for g in range(4):
                             zo = 4 * v + g - (oz - 1)
                             at = zo * C + 8 * j
-                            parts.append(product[t, at : at + 8, 128 * v : 128 * v + 128] if 1 <= zo <= 6 else None)
-                        halves.append(pick(group, parts))
-                    a.append(halves[0] + halves[1])
+                            parts.append(product[f, t, at : at + 8, 128 * v : 128 * v + 128] if 1 <= zo <= 6 else None)
+                        sides.append(pick(group, parts))
+                    a.append(sides[0] + sides[1])
                 pairs = [
                     jnp.where(odd, a[i + 1], a[i]) + pltpu.roll(jnp.where(odd, a[i], a[i + 1]), 32, 1) for i in (0, 2)
                 ]
@@ -337,21 +331,29 @@
                 pile[f, k // 4, 4 * (k % 4) + q] = (
                     tap_tile[f, source] if source < 27 else jnp.zeros((8, 128), F32)
                 )
-        return send(pile.at[f, 1 - rz], pair_in.at[f], (pair_send, pair_recv), f, (column[2], dp))
+        send(pile.at[f, 1 - rz], pair_in.at[f], (pair_send, pair_recv), f, (column[2], dp))
+        return batch(pair_in.at[f], (pair_send, pair_recv), f)
 
     loads[0].wait()
+    loads[1].wait()
+    flag = kept[...].astype(F32)
+    kept_cells = jnp.zeros((1, 256), F32)
+    for b in range(4):
+        kept_cells = jnp.where(tile == b, flag[:, b : b + 1], kept_cells)
     field = jnp.where(kept_cells > 0.5, vin[...].astype(F32).reshape(256, 256), GONE)
     field = turn_in(0, field)
     pl.semaphore_wait(barrier, len(greeted))
     volume_moves = give(0, 3, sel3[...], field)
 
-    send_rows(0, filter_one)
+    loads[2].wait()
+    loads[3].wait()
+    send_rows(0, rows_in.at[0])
     row_moves = [share_rows(0)]
-    send_rows(1, filter_two)
+    send_rows(1, rows_in.at[1])
     row_moves.append(share_rows(1))
 
     sel1[...] = faces_of(1)
-    loads[1].wait()
+    loads[4].wait()
     cot_moves = give(1, 1, sel1[...], turn_in(1, cin[...].astype(F32).reshape(256, 256)))
 
     rows3[...] = assemble(3)
@@ -387,8 +389,8 @@
     for b, value in enumerate(take(0, 3, rows3[...], volume_moves)):
         blk[b] = value
 
-    def first(r0):
-        rows = pl.ds(r0, 16)
+    def first(y):
+        rows = slice(16 * y, 16 * y + 16)
         here = inside[rows, :]
         for b in range(3):
             for v in range(2):
@@ -396,105 +398,115 @@
                 value = blk[b, rows, lanes]
                 kept_here = jnp.where(value == GONE, 0.0, here)
                 keep[b, rows, lanes] = kept_here
-                put(0, b, v, r0, value * kept_here)
-
-    tiles(19, first)
-    conv(0, 0, 18, False)
-
-    def second(r0):
-        rows = pl.ds(r0, 16)
+                put(0, b, v, 16 * y, value * kept_here)
+
+    def second(y):
+        rows = slice(16 * y, 16 * y + 16)
         parts = []
         for b in range(3):
-            parts.append([])
-            for v in range(2):
-                lanes = slice(128 * v, 128 * v + 128)
-                value, there = pre[b, rows, lanes], keep[b, rows, lanes]
-                gate = logistic(value)
-                slope[b, rows, lanes] = (gate + value * gate * (1.0 - gate)) * there
-                parts[b].append(value * gate * there)
-        put_all(1, r0, parts)
-
-    tiles(18, second)
-    conv(1, 1, 17, False)
-    for b, value in enumerate(take(1, 1, rows1[...], cot_moves)):
-        cot[b] = value
+            value, there = pre[0, b, rows, :], keep[b, rows, :]
+            gate = logistic(value)
+            act = value * gate
+            slope[b, rows, :] = (gate + act * (1.0 - gate)) * there
+            parts.append(halves(act * there))
+        put_all(1, 16 * y, parts)
+
     x = iota((16, 128), 0) - 4
     own = [jnp.where((x >= 0) & (x < 8), 1.0, 0.0)]
     own.append(jnp.where(group == 0, own[0], 0.0))
-
-    def third(r0, last=False):
-        rows = pl.ds(r0, 16)
+    own_lanes = [jnp.concatenate([own[0], own[b // 2]], axis=1) for b in range(3)]
+
+    def third(y):
+        rows = slice(16 * y, 16 * y + 16)
         parts = []
         for b in range(3):
-            parts.append([])
-            for v in range(2):
-                lanes = slice(128 * v, 128 * v + 128)
-                value, there = pre[b, rows, lanes], keep[b, rows, lanes]
-                gate = logistic(value)
-                grad = cot[b, rows, lanes] * there * (gate + value * gate * (1.0 - gate))
-                parts[b].append(grad)
-                if not last:
-                    leaving[b, rows, lanes] = (value * gate * there).astype(BF16)
-                    owned[1, b, rows, lanes] = (grad * own[b * v // 2]).astype(BF16)
-        put_all(2, r0, parts)
-
-    tiles(16, third, 2)
-    third(256, True)
-    conv(2, 3, 16, True)
-
-    def fourth(r0):
-        rows = pl.ds(r0, 16)
+            value, there = pre[1, b, rows, :], keep[b, rows, :]
+            gate = logistic(value)
+            act = value * gate
+            grad = cot[b, rows, :] * there * (gate + act * (1.0 - gate))
+            parts.append(halves(grad))
+            if y < 16:
+                leaving[b, rows, :] = (act * there).astype(BF16)
+                owned[1, b, rows, :] = (grad * own_lanes[b]).astype(BF16)
+        put_all(2, 16 * y, parts)
+
+    def fourth(y):
+        rows = slice(16 * y, 16 * y + 16)
         for b in range(3):
-            for v in range(2):
-                lanes = slice(128 * v, 128 * v + 128)
-                grad = pre[b, rows, lanes] * slope[b, rows, lanes]
-                owned[0, b, rows, lanes] = (grad * own[b * v // 2]).astype(BF16)
-
-    tiles(16, fourth, 2)
+            owned[0, b, rows, :] = (pre[3, b, rows, :] * slope[b, rows, :] * own_lanes[b]).astype(BF16)
+
+    def run(body, first_y, end):
+        for y in range(first_y, end):
+            body(y)
+
+    run(first, 0, 8)
+    conv(0, 0, False, 0, 6)
+    run(first, 8, 14)
+    conv(0, 0, False, 6, 6)
+    run(second, 0, 6)
+    run(first, 14, 19)
+    conv(0, 0, False, 12, 6)
+    run(second, 6, 12)
+    conv(1, 1, False, 0, 6)
+    run(second, 12, 18)
+    conv(1, 1, False, 6, 6)
+    for b, value in enumerate(take(1, 1, rows1[...], cot_moves)):
+        cot[b] = value
+    run(third, 0, 6)
+    conv(1, 1, False, 12, 5)
+    run(third, 6, 12)
+    conv(2, 3, True, 0, 6)
+    run(third, 12, 17)
+    conv(2, 3, True, 6, 5)
+    run(fourth, 0, 6)
+    conv(2, 3, True, 11, 5)
+    run(fourth, 6, 16)
+    pair_one = filter_gradient(0, 0)
     pair_two = filter_gradient(1, 1)
-    pair_one = filter_gradient(0, 0)
     grad_moves = give(2, 1, sel1[...], natural(owned[0]).astype(BF16))
-    for f, move in ((1, pair_two), (0, pair_one)):
+    for f, move in ((0, pair_one), (1, pair_two)):
         move.wait_recv()
         for s in range(16):
             crossing[s, f] = pile[f, rz, s] + pair_in[f, s]
-    xy_moves = [
-        send(crossing.at[s], xy_in.at[xy], (xy_send, xy_recv), i, peer)
-        for i, (s, peer) in enumerate(zip(xy_slots, xy_peers))
-    ]
+    for s, peer in zip(xy_slots, xy_peers):
+        send(crossing.at[s], xy_in.at[xy], (xy_send, xy_recv), 0, peer)
+    xy_moves = [batch(xy_in.at[0:15], (xy_send, xy_recv), 0)]
     xy_in[xy] = crossing[xy]
 
-    outs = [depart(0, natural(leaving[...]), act_out)]
+    depart(natural(leaving[...]), act_out)
     for move in xy_moves:
         move.wait_recv()
     total = xy_in[0]
     for s in range(1, 16):
         total = total + xy_in[s]
     z_in[pz] = total
-    z_moves = [
-        send(z_in.at[pz], z_in.at[pz], (z_send, z_recv), i, peer) for i, peer in enumerate(z_peers)
-    ]
+    for peer in z_peers:
+        send(z_in.at[pz], z_in.at[pz], (z_send, z_recv), 0, peer)
+    z_moves = [batch(z_in.at[0:7], (z_send, z_recv), 0)]
 
     for b, value in enumerate(take(2, 1, rows1[...], grad_moves)):
         blk[b] = value
 
-    def fifth(r0):
-        rows = pl.ds(r0, 16)
+    def fifth(y):
+        rows = slice(16 * y, 16 * y + 16)
         here = inside[rows, :]
         for b in range(3):
             for v in range(2):
-                put(3, b, v, r0, blk[b, rows, 128 * v : 128 * v + 128] * here)
-
-    tiles(17, fifth, 2)
-    conv(3, 2, 16, True)
-
-    def sixth(r0):
-        rows = pl.ds(r0, 16)
+                put(3, b, v, 16 * y, blk[b, rows, 128 * v : 128 * v + 128] * here)
+
+    def sixth(y):
+        rows = slice(16 * y, 16 * y + 16)
         for b in range(3):
-            leaving[b, rows, :] = (pre[b, rows, :] * keep[b, rows, :]).astype(BF16)
-
-    tiles(16, sixth, 2)
-    outs.append(depart(1, natural(leaving[...]), gin_out))
+            leaving[b, rows, :] = (pre[2, b, rows, :] * keep[b, rows, :]).astype(BF16)
+
+    run(fifth, 0, 8)
+    conv(3, 2, True, 0, 6)
+    run(fifth, 8, 17)
+    conv(3, 2, True, 6, 5)
+    run(sixth, 0, 6)
+    conv(3, 2, True, 11, 5)
+    run(sixth, 6, 16)
+    depart(natural(leaving[...]), gin_out)
 
     for move in z_moves:
         move.wait_recv()
@@ -502,9 +514,9 @@
     for s in range(1, 8):
         total = total + z_in[s]
     xc_in[xc] = total * (1.0 / math.sqrt(4 * count * 2048))
-    xc_moves = [
-        send(xc_in.at[xc], xc_in.at[xc], (xc_send, xc_recv), i, peer) for i, peer in enumerate(xc_peers)
-    ]
+    for peer in xc_peers:
+        send(xc_in.at[xc], xc_in.at[xc], (xc_send, xc_recv), 0, peer)
+    xc_moves = [batch(xc_in.at[0:7], (xc_send, xc_recv), 0)]
     for move in xc_moves:
         move.wait_recv()
     offset = lax.rem(4 - dp, 4) * 8
@@ -518,27 +530,34 @@
                 final[8 * j : 8 * j + 8, 128 * w : 128 * w + 128] = pick(group, parts)
         out[...] = pltpu.roll(final[...], 256 - offset, 1)[:, :216]
 
-    for copy in outs:
-        copy.wait()
     for copy in started:
         copy.wait_send()
+
+
+def hand_over(*refs):
+    copies = [pltpu.make_async_copy(refs[i], refs[4 + i], refs[8].at[i]) for i in range(4)]
+    for copy in copies:
+        copy.start()
+    for copy in copies:
+        copy.wait()
 
 
 def on_device(volume, tissue_kept, filter_one, filter_two, cotangent):
     vmem, anywhere = pl.BlockSpec(memory_space=pltpu.VMEM), pl.BlockSpec(memory_space=pl.ANY)
     dma = pltpu.SemaphoreType.DMA
-    field = jax.ShapeDtypeStruct(volume.shape, BF16)
-    grad = jax.ShapeDtypeStruct((C, 216), F32)
+    field, grad = (volume.shape, BF16), ((C, 216), F32)
+    results = (field, field, grad, grad)
     blocked = pltpu.VMEM((3, 304, 256), F32)
-    act, gin, one, two = pl.pallas_call(
+    held = pl.pallas_call(
         kernel,
-        out_shape=(field, field, grad, grad),
-        in_specs=[pl.BlockSpec(memory_space=pltpu.SMEM), vmem, vmem, anywhere, anywhere],
-        out_specs=(anywhere, anywhere, vmem, vmem),
+        out_shape=tuple(pltpu.VMEM(*r) for r in results),
+        in_specs=[anywhere] * 5,
+        out_specs=(vmem,) * 4,
         scratch_shapes=[
+            pltpu.VMEM((1, 4), jnp.int32),
+            pltpu.VMEM((2, C, 216), BF16),
             pltpu.VMEM((C, 8, 256), BF16),
             pltpu.VMEM((C, 8, 256), BF16),
-            pltpu.VMEM((2, C, 8, 256), BF16),
             pltpu.VMEM((256, 1024), F32),
             pltpu.VMEM((5, 128, 128), F32),
             pltpu.VMEM((3, 128, 512), BF16),
@@ -551,7 +570,7 @@
             blocked,
             blocked,
             blocked,
-            blocked,
+            pltpu.VMEM((4, 3, 288, 256), F32),
             pltpu.VMEM((4, 3, 3, 320, 256), BF16),
             pltpu.VMEM((4, 9, 256, 256), BF16),
             pltpu.VMEM((3, 256, 256), BF16),
@@ -561,7 +580,7 @@
             pltpu.VMEM((2, 4, 64, 128), BF16),
             pltpu.VMEM((864, 128), F32),
             pltpu.VMEM((2, 27, C, 128), F32),
-            pltpu.VMEM((9, 256, 256), F32),
+            pltpu.VMEM((2, 9, 256, 256), F32),
             pltpu.VMEM((2, 27, 8, 128), F32),
             pltpu.VMEM((2, 2, 16, 8, 128), F32),
             pltpu.VMEM((2, 16, 8, 128), F32),
@@ -582,13 +601,20 @@
             pltpu.VMEM((128, 256), BF16),
             pltpu.VMEM((768, 640), BF16),
             pltpu.VMEM((304, 128), F32),
-            dma((2,)), dma((2,)), dma((3, 11)), dma((3, 11)), dma((2, 3)), dma((2, 3)),
-            dma((2,)), dma((2,)), dma((15,)), dma((15,)), dma((7,)), dma((7,)), dma((7,)), dma((7,)),
+            dma((5,)), dma((3, 2)), dma((3, 2)), dma((2,)), dma((2,)),
+            dma((2,)), dma((2,)), dma((1,)), dma((1,)), dma((1,)), dma((1,)), dma((1,)), dma((1,)),
         ],
         compiler_params=pltpu.CompilerParams(
-            collective_id=0, has_side_effects=True, vmem_limit_bytes=48 * 1024 * 1024
+            collective_id=0, has_side_effects=True, vmem_limit_bytes=60 * 1024 * 1024
         ),
     )(tissue_kept, filter_one.T, filter_two.T, volume, cotangent)
+    act, gin, one, two = pl.pallas_call(
+        hand_over,
+        out_shape=tuple(jax.ShapeDtypeStruct(*r) for r in results),
+        in_specs=[anywhere] * 4,
+        out_specs=(anywhere,) * 4,
+        scratch_shapes=[dma((4,))],
+    )(*(pltpu.with_memory_space_constraint(part, pltpu.VMEM) for part in held))
     return act, gin, one.T, two.T
 
 

time: 56.5 us -> 43.8 us (0.78)
  local copies, waits for them, and re-layouts: 6.43 us -> 0 us
  Pallas kernels: 49.1 us -> 43 us
    unnamed x14 -> x0, local copies, waits for them, and re-layouts: 6.43 us -> none
    pallas_call x1 -> x2, Pallas kernels: 49.1 us -> 43 us  [the longest x1 42.3 us: on_device(): pl.pallas_call(kernel, out_shape=tuple((pltpu.VMEM(*r) for r in results))...]
where the time goes in v3:
time: 43.8 us; the launch traced here: 43.7 us
  Pallas kernels  43 us (98%)
  between operations  0.64 us (1%)
    pallas_call x1, Pallas kernels, on_device(): pl.pallas_call(kernel, out_shape=tuple((pltpu.VMEM(*r) for r in results))...  42.3 us

profile of v3, /device:TPU:1, one launch (start us, length us, event | category | flops | bytes accessed | tf_op | source)
XLA Modules:
  0.0 43.7 jit_solution(11161754309930385722)
XLA Ops:
  0.6 42.3 %shard_map.84 = (bf16[1,1,32,8,256]{4,3,2,1,0:T(8,128)(2,1)S(1)}, bf16[1,1,32,8,256]{4,3,2,1,0:T(8,128)(2,1)S(1)}, f32[32,216]{1,0:T(8,128)S(1)}, f32[32,216]{1,0:T(8,128)S(1)}) custom-call(s32[1,1,4]{2,1,0:T(1,128)} %flags.1, bf16[32,216]{1,0:T(8,128)(2,1)} %bitcast.4, bf16[32,216]{1,0:T(8,128)(2,1)} %bitcast.5, bf16[1,1,32,8,256]{4,3,2,1,0:T(8,128)(2,1)} %volume.1, ...), custom_call_target="tpu_custom_call" | custom-call | tf_op jit(solution)/shard_map/pallas_call | solution.py:551
  42.9 0.7 %shard_map.85 = (bf16[1,1,32,8,256]{4,3,2,1,0:T(8,128)(2,1)}, bf16[1,1,32,8,256]{4,3,2,1,0:T(8,128)(2,1)}, f32[32,216]{1,0:T(8,128)}, f32[32,216]{1,0:T(8,128)}) custom-call(bf16[1,1,32,8,256]{4,3,2,1,0:T(8,128)(2,1)S(1)} %get-tuple-element.12.refs_0_, bf16[1,1,32,8,256]{4,3,2,1,0:T(8,128)(2,1)S(1)} %get-tuple-element.13.refs_1_, ...), custom_call_target="tpu_custom_call" | custom-call | tf_op jit(solution)/shard_map/pallas_call | solution.py:611

commit v4 on v3

--- a/solution.py
+++ b/solution.py
@@ -58,7 +58,7 @@
     kept, rows_in, vin, cin, spread, nat, nat_main, nat_z, face_main, face_z, stack_main, stack_z,
     blk, cot, keep, slope, pre, shifted, bands, leaving, owned, wide,
     wsend, wrecv, wrows, rep, product, tap_tile, pile, pair_in, crossing, xy_in, z_in, xc_in, final,
-    turn, copies8, sel3, sel1, rows3, rows1, place0, place1, place2, pack, unplace, inside,
+    turn, copies8, sel3, sel1, near3, far3, near1, far1, place0, place1, place2, pack, unplace, inside,
     local_sem, halo_send, halo_recv, filt_send, filt_recv,
     pair_send, pair_recv, xy_send, xy_recv, z_send, z_recv, xc_send, xc_recv,
 ):
@@ -143,15 +143,18 @@
                 nat[w, pl.ds(x, 16, stride=8), :] = pick(group, parts)
         return jnp.concatenate([nat[w] for w in range(5)], axis=1).astype(BF16)
 
-    def give(f, h, sel, field):
-        yrows, low, high, beyond, corner_low, corner_high, total = layout(h)
+    def show(f, h, sel, field):
         main, last = field[:, :512], field[:, 512:]
         nat_main[f] = main
         nat_z[f] = last
+        stack_main[f, 0:128] = main
         faces = dot(sel, field).astype(BF16)
         for side in range(2):
             face_main[f, side, 0 : 16 * h] = faces[16 * h * side : 16 * h * side + 16 * h, :512]
             face_z[f, side, 0 : 16 * h] = faces[16 * h * side : 16 * h * side + 16 * h, 512:]
+
+    def give(f, h):
+        yrows, low, high, beyond, corner_low, corner_high, total = layout(h)
         sems = (halo_send, halo_recv)
 
         def add(src, dst, d, kind):
@@ -160,41 +163,47 @@
         ends = ((1, low, corner_low, above), (0, high, corner_high, below))
         for side, at, _, to in ends:
             add(face_main.at[f, side, 0 : 16 * h], stack_main.at[f, at : at + 16 * h], to[0], 0)
-        for side, at, corner, to in ends:
+        for side, at, _, to in ends:
             add(face_z.at[f, side, 0 : 16 * h], stack_z.at[f, at : at + 16 * h], to[2], 1)
-            add(face_main.at[f, side, 16 * h - 16 : 16 * h], stack_main.at[f, corner : corner + 16], to[1], 0)
-            add(face_z.at[f, side, 16 * h - 16 : 16 * h], stack_z.at[f, corner : corner + 16], to[3], 1)
-        add(nat_main.at[f, 128 - yrows : 128], stack_main.at[f, beyond : beyond + yrows], column[1], 0)
-        add(nat_z.at[f, 128 - yrows : 128], stack_z.at[f, beyond : beyond + yrows], column[3], 1)
         add(nat_z.at[f], stack_z.at[f, 0:128], column[2], 1)
-        stack_main[f, 0:128] = main
-        return [batch(stack_main.at[f, 128:total], sems, (f, 0)), batch(stack_z.at[f, 0:total], sems, (f, 1))]
+        for side, _, corner, to in ends:
+            add(face_main.at[f, side, 16 * h - 16 : 16 * h], stack_main.at[f, corner : corner + 16], to[1], 2)
+            add(face_z.at[f, side, 16 * h - 16 : 16 * h], stack_z.at[f, corner : corner + 16], to[3], 3)
+        add(nat_main.at[f, 128 - yrows : 128], stack_main.at[f, beyond : beyond + yrows], column[1], 2)
+        add(nat_z.at[f, 128 - yrows : 128], stack_z.at[f, beyond : beyond + yrows], column[3], 3)
+        near = [batch(stack_main.at[f, 128:beyond], sems, (f, 0)), batch(stack_z.at[f, 0:beyond], sems, (f, 1))]
+        far = [
+            batch(stack_main.at[f, beyond:total], sems, (f, 2)), batch(stack_z.at[f, beyond:total], sems, (f, 3))
+        ]
+        return near, far
 
     def assemble(h):
         yrows, low, high, beyond, corner_low, corner_high, total = layout(h)
-        row, col = iota((304, total), 0), iota((304, total), 1)
+        row, col = iota((256, beyond), 0), iota((256, beyond), 1)
         y, x = row // 16, row % 16 - 4
-        mid, lo, hi = (x >= 0) & (x < 8), (x < 0) & (x >= -h), (x >= 8) & (x < 8 + h)
-        own, far = y < 16, (y >= 16) & (y < 16 + h)
-        first, there = 16 - yrows // 8, 31 - y
-        skip = 16 * h - 16
-        at = jnp.where(own & mid, 8 * y + x, -1)
-        at = jnp.where(own & lo, low + h * y + x + h, at)
-        at = jnp.where(own & hi, high + h * y + x - 8, at)
-        at = jnp.where(far & mid, beyond + 8 * (there - first) + x, at)
-        at = jnp.where(far & lo, corner_low + h * there + x + h - skip, at)
-        at = jnp.where(far & hi, corner_high + h * there + x - 8 - skip, at)
-        return ones_at(at == col)
-
-    def take(f, h, rows, moves):
+        at = jnp.where((x >= 0) & (x < 8), 8 * y + x, -1)
+        at = jnp.where((x < 0) & (x >= -h), low + h * y + x + h, at)
+        at = jnp.where((x >= 8) & (x < 8 + h), high + h * y + x - 8, at)
+        near = ones_at(at == col)
+        row, col = iota((48, total - beyond), 0), iota((48, total - beyond), 1)
+        y, x = row // 16, row % 16 - 4
+        there, skip = 15 - y, 16 * h - 16
+        at = jnp.where((x >= 0) & (x < 8), 8 * (there - (16 - yrows // 8)) + x, -1)
+        at = jnp.where((x < 0) & (x >= -h), yrows + h * there + x + h - skip, at)
+        at = jnp.where((x >= 8) & (x < 8 + h), yrows + 16 + h * there + x - 8 - skip, at)
+        return near, ones_at((at == col) & (y < h))
+
+    def take(f, h, rows, part, moves, into):
         for move in moves:
             move.wait_recv()
-        total = layout(h)[-1]
-        pieces = jnp.concatenate([stack_main[f, 0:total], stack_z[f, 0:total]], axis=1)
-        whole = dot(rows, pieces).astype(BF16)
-        return (
-            dot(whole[:, 0:256], place0[...]), dot(whole[:, 128:512], place1[...]), dot(whole[:, 256:640], place2[...])
-        )
+        beyond, total = layout(h)[3], layout(h)[-1]
+        start, end = ((0, beyond), (beyond, total))[part]
+        pieces = jnp.concatenate([stack_main[f, start:end], stack_z[f, start:end]], axis=1)
+        whole = dot(rows[...], pieces).astype(BF16)
+        to = slice(256 * part, 256 + 48 * part)
+        into[0, to] = dot(whole[:, 0:256], place0[...])
+        into[1, to] = dot(whole[:, 128:512], place1[...])
+        into[2, to] = dot(whole[:, 256:640], place2[...])
 
     def halves(value):
         return value[:, :128], value[:, 128:]
@@ -342,27 +351,26 @@
         kept_cells = jnp.where(tile == b, flag[:, b : b + 1], kept_cells)
     field = jnp.where(kept_cells > 0.5, vin[...].astype(F32).reshape(256, 256), GONE)
     field = turn_in(0, field)
-    pl.semaphore_wait(barrier, len(greeted))
-    volume_moves = give(0, 3, sel3[...], field)
-
+    show(0, 3, sel3[...], field)
     loads[2].wait()
     loads[3].wait()
     send_rows(0, rows_in.at[0])
-    row_moves = [share_rows(0)]
     send_rows(1, rows_in.at[1])
-    row_moves.append(share_rows(1))
-
-    sel1[...] = faces_of(1)
-    loads[4].wait()
-    cot_moves = give(1, 1, sel1[...], turn_in(1, cin[...].astype(F32).reshape(256, 256)))
-
-    rows3[...] = assemble(3)
-    rows1[...] = assemble(1)
+    pl.semaphore_wait(barrier, len(greeted))
+    volume_near, volume_far = give(0, 3)
+    row_moves = [share_rows(0), share_rows(1)]
+
+    near3[...], far3[...] = assemble(3)
     k, n = iota((256, 256), 0), iota((256, 256), 1)
     place0[...] = ones_at(n - k == C)
     k, n = iota((384, 256), 0), iota((384, 256), 1)
     place1[...] = ones_at(k - n == C)
     place2[...] = ones_at(k - n == jnp.where(n < 160, 96, 128))
+    sel1[...] = faces_of(1)
+    loads[4].wait()
+    show(1, 1, sel1[...], turn_in(1, cin[...].astype(F32).reshape(256, 256)))
+    cot_near, cot_far = give(1, 1)
+    near1[...], far1[...] = assemble(1)
     row, col = iota((128, 256), 0), iota((128, 256), 1)
     pack[...] = ones_at(col == 16 * (row // 8) + row % 8 + 4)
     for b in range(3):
@@ -386,8 +394,7 @@
         band(f)
         band_back(f)
 
-    for b, value in enumerate(take(0, 3, rows3[...], volume_moves)):
-        blk[b] = value
+    take(0, 3, near3, 0, volume_near, blk)
 
     def first(y):
         rows = slice(16 * y, 16 * y + 16)
@@ -441,29 +448,32 @@
 
     run(first, 0, 8)
     conv(0, 0, False, 0, 6)
-    run(first, 8, 14)
+    run(first, 8, 16)
     conv(0, 0, False, 6, 6)
     run(second, 0, 6)
-    run(first, 14, 19)
+    take(0, 3, far3, 1, volume_far, blk)
+    run(first, 16, 19)
     conv(0, 0, False, 12, 6)
     run(second, 6, 12)
     conv(1, 1, False, 0, 6)
     run(second, 12, 18)
     conv(1, 1, False, 6, 6)
-    for b, value in enumerate(take(1, 1, rows1[...], cot_moves)):
-        cot[b] = value
+    take(1, 1, near1, 0, cot_near, cot)
     run(third, 0, 6)
     conv(1, 1, False, 12, 5)
     run(third, 6, 12)
     conv(2, 3, True, 0, 6)
-    run(third, 12, 17)
+    run(third, 12, 16)
+    take(1, 1, far1, 1, cot_far, cot)
+    run(third, 16, 17)
     conv(2, 3, True, 6, 5)
     run(fourth, 0, 6)
     conv(2, 3, True, 11, 5)
     run(fourth, 6, 16)
     pair_one = filter_gradient(0, 0)
     pair_two = filter_gradient(1, 1)
-    grad_moves = give(2, 1, sel1[...], natural(owned[0]).astype(BF16))
+    show(2, 1, sel1[...], natural(owned[0]).astype(BF16))
+    grad_near, grad_far = give(2, 1)
     for f, move in ((0, pair_one), (1, pair_two)):
         move.wait_recv()
         for s in range(16):
@@ -479,13 +489,12 @@
     total = xy_in[0]
     for s in range(1, 16):
         total = total + xy_in[s]
-    z_in[pz] = total
+    z_in[pz] = total.reshape(16, 128).astype(BF16)
     for peer in z_peers:
         send(z_in.at[pz], z_in.at[pz], (z_send, z_recv), 0, peer)
     z_moves = [batch(z_in.at[0:7], (z_send, z_recv), 0)]
 
-    for b, value in enumerate(take(2, 1, rows1[...], grad_moves)):
-        blk[b] = value
+    take(2, 1, near1, 0, grad_near, blk)
 
     def fifth(y):
         rows = slice(16 * y, 16 * y + 16)
@@ -501,19 +510,21 @@
 
     run(fifth, 0, 8)
     conv(3, 2, True, 0, 6)
-    run(fifth, 8, 17)
+    run(fifth, 8, 16)
     conv(3, 2, True, 6, 5)
     run(sixth, 0, 6)
+    take(2, 1, far1, 1, grad_far, blk)
+    run(fifth, 16, 17)
     conv(3, 2, True, 11, 5)
     run(sixth, 6, 16)
     depart(natural(leaving[...]), gin_out)
 
     for move in z_moves:
         move.wait_recv()
-    total = z_in[0]
+    total = z_in[0].astype(F32)
     for s in range(1, 8):
-        total = total + z_in[s]
-    xc_in[xc] = total * (1.0 / math.sqrt(4 * count * 2048))
+        total = total + z_in[s].astype(F32)
+    xc_in[xc] = (total * (1.0 / math.sqrt(4 * count * 2048))).astype(BF16)
     for peer in xc_peers:
         send(xc_in.at[xc], xc_in.at[xc], (xc_send, xc_recv), 0, peer)
     xc_moves = [batch(xc_in.at[0:7], (xc_send, xc_recv), 0)]
@@ -525,7 +536,7 @@
             for w in range(2):
                 parts = []
                 for g in range(4):
-                    value = xc_in[4 * w + g, f]
+                    value = xc_in[4 * w + g].astype(F32)[8 * f : 8 * f + 8]
                     parts.append(value if g == j else pltpu.roll(value, 32 * ((g - j) % 4), 1))
                 final[8 * j : 8 * j + 8, 128 * w : 128 * w + 128] = pick(group, parts)
         out[...] = pltpu.roll(final[...], 256 - offset, 1)[:, :216]
@@ -586,22 +597,24 @@
             pltpu.VMEM((2, 16, 8, 128), F32),
             pltpu.VMEM((16, 2, 8, 128), F32),
             pltpu.VMEM((16, 2, 8, 128), F32),
-            pltpu.VMEM((8, 2, 8, 128), F32),
-            pltpu.VMEM((8, 2, 8, 128), F32),
+            pltpu.VMEM((8, 16, 128), BF16),
+            pltpu.VMEM((8, 16, 128), BF16),
             pltpu.VMEM((C, 256), F32),
             pltpu.VMEM((256, 256), BF16),
             pltpu.VMEM((256, 1024), BF16),
             pltpu.VMEM((96, 128), BF16),
             pltpu.VMEM((32, 128), BF16),
-            pltpu.VMEM((304, 288), BF16),
-            pltpu.VMEM((304, 208), BF16),
+            pltpu.VMEM((256, 224), BF16),
+            pltpu.VMEM((48, 64), BF16),
+            pltpu.VMEM((256, 160), BF16),
+            pltpu.VMEM((48, 48), BF16),
             pltpu.VMEM((256, 256), BF16),
             pltpu.VMEM((384, 256), BF16),
             pltpu.VMEM((384, 256), BF16),
             pltpu.VMEM((128, 256), BF16),
             pltpu.VMEM((768, 640), BF16),
             pltpu.VMEM((304, 128), F32),
-            dma((5,)), dma((3, 2)), dma((3, 2)), dma((2,)), dma((2,)),
+            dma((5,)), dma((3, 4)), dma((3, 4)), dma((2,)), dma((2,)),
             dma((2,)), dma((2,)), dma((1,)), dma((1,)), dma((1,)), dma((1,)), dma((1,)), dma((1,)),
         ],
         compiler_params=pltpu.CompilerParams(

time: 43.8 us -> 42.4 us (0.968)
  Pallas kernels: 43 us -> 41.6 us
    pallas_call x1, Pallas kernels: 42.3 us -> 40.9 us  [on_device(): pl.pallas_call(kernel, out_shape=tuple((pltpu.VMEM(*r) for r in results))...]
where the time goes in v4:
time: 42.4 us; the launch traced here: 42.3 us
  Pallas kernels  41.6 us (98%)
  between operations  0.64 us (2%)
    pallas_call x1, Pallas kernels, on_device(): pl.pallas_call(kernel, out_shape=tuple((pltpu.VMEM(*r) for r in results))...  40.9 us

profile of v4, /device:TPU:1, one launch (start us, length us, event | category | flops | bytes accessed | tf_op | source)
XLA Modules:
  0.0 42.3 jit_solution(6459585645048180319)
XLA Ops:
  0.6 40.9 %shard_map.84 = (bf16[1,1,32,8,256]{4,3,2,1,0:T(8,128)(2,1)S(1)}, bf16[1,1,32,8,256]{4,3,2,1,0:T(8,128)(2,1)S(1)}, f32[32,216]{1,0:T(8,128)S(1)}, f32[32,216]{1,0:T(8,128)S(1)}) custom-call(s32[1,1,4]{2,1,0:T(1,128)} %flags.1, bf16[32,216]{1,0:T(8,128)(2,1)} %bitcast.4, bf16[32,216]{1,0:T(8,128)(2,1)} %bitcast.5, bf16[1,1,32,8,256]{4,3,2,1,0:T(8,128)(2,1)} %volume.1, ...), custom_call_target="tpu_custom_call" | custom-call | tf_op jit(solution)/shard_map/pallas_call | solution.py:562
  41.5 0.7 %shard_map.85 = (bf16[1,1,32,8,256]{4,3,2,1,0:T(8,128)(2,1)}, bf16[1,1,32,8,256]{4,3,2,1,0:T(8,128)(2,1)}, f32[32,216]{1,0:T(8,128)}, f32[32,216]{1,0:T(8,128)}) custom-call(bf16[1,1,32,8,256]{4,3,2,1,0:T(8,128)(2,1)S(1)} %get-tuple-element.12.refs_0_, bf16[1,1,32,8,256]{4,3,2,1,0:T(8,128)(2,1)S(1)} %get-tuple-element.13.refs_1_, ...), custom_call_target="tpu_custom_call" | custom-call | tf_op jit(solution)/shard_map/pallas_call | solution.py:624

commit v5 on v4

--- a/solution.py
+++ b/solution.py
@@ -42,6 +42,11 @@
     return value
 
 
+def x_of(row):
+    x = row % 16
+    return jnp.where(x < 12, x, x - 16)
+
+
 def logistic(v):
     return 1.0 / (1.0 + jnp.exp(-v))
 
@@ -56,9 +61,9 @@
     flags, filter_one, filter_two, volume, cotangent,
     act_out, gin_out, grad_one_out, grad_two_out,
     kept, rows_in, vin, cin, spread, nat, nat_main, nat_z, face_main, face_z, stack_main, stack_z,
-    blk, cot, keep, slope, pre, shifted, bands, leaving, owned, wide,
+    blk, cot, keep, slope, pre, back, shifted, packed, bands, leaving, owned, wide,
     wsend, wrecv, wrows, rep, product, tap_tile, pile, pair_in, crossing, xy_in, z_in, xc_in, final,
-    turn, copies8, sel3, sel1, near3, far3, near1, far1, place0, place1, place2, pack, unplace, inside,
+    turn, copies8, sel3, sel1, near3, far3, near1, far1, place0, place1, place2, unplace, inside,
     local_sem, halo_send, halo_recv, filt_send, filt_recv,
     pair_send, pair_recv, xy_send, xy_recv, z_send, z_recv, xc_send, xc_recv,
 ):
@@ -99,11 +104,14 @@
     below = [lax.rem(d - 4 + count, count) for d in column]
     above = [lax.rem(d + 4, count) for d in column]
     xy = bx * 4 + dp
-    xy_slots = [lax.rem(xy + k, 16) for k in range(1, 16)]
+    hops = lambda d: min(d, 4 - d)
+    steps = sorted([(i // 4, i % 4) for i in range(1, 16)], key=lambda d: -hops(d[0]) - hops(d[1]))
+    xy_slots = [lax.rem(bx + i, 4) * 4 + lax.rem(dp + j, 4) for i, j in steps]
     xy_peers = [((s // 4) * 16 + lax.rem(space, 16), s % 4) for s in xy_slots]
-    z_peers = [(bx * 16 + 2 * lax.rem(pz + k, 8) + rz, dp) for k in range(1, 8)]
+    z_peers = [(bx * 16 + 2 * lax.rem(pz + k, 8) + rz, dp) for k in (4, 3, 5, 2, 6, 1, 7)]
     xc = rz * 4 + bx
-    xc_slots = [lax.rem(xc + k, 8) for k in range(1, 8)]
+    steps = ((1, 2), (0, 2), (1, 1), (1, 3), (0, 1), (0, 3), (1, 0))
+    xc_slots = [lax.rem(rz + i, 2) * 4 + lax.rem(bx + j, 4) for i, j in steps]
     xc_peers = [((s % 4) * 16 + 2 * pz + s // 4, dp) for s in xc_slots]
     dp_peers = [(space, lax.rem(dp + k, 4)) for k in range(1, 4)]
 
@@ -162,13 +170,14 @@
 
         ends = ((1, low, corner_low, above), (0, high, corner_high, below))
         for side, at, _, to in ends:
+            add(face_z.at[f, side, 0 : 16 * h], stack_z.at[f, at : at + 16 * h], to[2], 1)
+        for side, _, corner, to in ends:
+            add(face_z.at[f, side, 16 * h - 16 : 16 * h], stack_z.at[f, corner : corner + 16], to[3], 3)
+        for side, at, _, to in ends:
             add(face_main.at[f, side, 0 : 16 * h], stack_main.at[f, at : at + 16 * h], to[0], 0)
-        for side, at, _, to in ends:
-            add(face_z.at[f, side, 0 : 16 * h], stack_z.at[f, at : at + 16 * h], to[2], 1)
-        add(nat_z.at[f], stack_z.at[f, 0:128], column[2], 1)
         for side, _, corner, to in ends:
             add(face_main.at[f, side, 16 * h - 16 : 16 * h], stack_main.at[f, corner : corner + 16], to[1], 2)
-            add(face_z.at[f, side, 16 * h - 16 : 16 * h], stack_z.at[f, corner : corner + 16], to[3], 3)
+        add(nat_z.at[f], stack_z.at[f, 0:128], column[2], 1)
         add(nat_main.at[f, 128 - yrows : 128], stack_main.at[f, beyond : beyond + yrows], column[1], 2)
         add(nat_z.at[f, 128 - yrows : 128], stack_z.at[f, beyond : beyond + yrows], column[3], 3)
         near = [batch(stack_main.at[f, 128:beyond], sems, (f, 0)), batch(stack_z.at[f, 0:beyond], sems, (f, 1))]
@@ -180,13 +189,13 @@
     def assemble(h):
         yrows, low, high, beyond, corner_low, corner_high, total = layout(h)
         row, col = iota((256, beyond), 0), iota((256, beyond), 1)
-        y, x = row // 16, row % 16 - 4
+        y, x = row // 16, x_of(row)
         at = jnp.where((x >= 0) & (x < 8), 8 * y + x, -1)
         at = jnp.where((x < 0) & (x >= -h), low + h * y + x + h, at)
         at = jnp.where((x >= 8) & (x < 8 + h), high + h * y + x - 8, at)
         near = ones_at(at == col)
         row, col = iota((48, total - beyond), 0), iota((48, total - beyond), 1)
-        y, x = row // 16, row % 16 - 4
+        y, x = row // 16, x_of(row)
         there, skip = 15 - y, 16 * h - 16
         at = jnp.where((x >= 0) & (x < 8), 8 * (there - (16 - yrows // 8)) + x, -1)
         at = jnp.where((x < 0) & (x >= -h), yrows + h * there + x + h - skip, at)
@@ -208,40 +217,52 @@
     def halves(value):
         return value[:, :128], value[:, 128:]
 
-    def put(f, b, v, r0, value):
+    last_own = {}
+
+    def put(f, b, v, y, value):
         lanes = slice(128 * v, 128 * v + 128)
-        at = slice(r0 + 16, r0 + 32)
-        shifted[f, 1, b, at, lanes] = value.astype(BF16)
-        shifted[f, 0, b, at, lanes] = pltpu.roll(value, 1, 0).astype(BF16)
-        shifted[f, 2, b, at, lanes] = pltpu.roll(value, 15, 0).astype(BF16)
-
-    def put_all(f, r0, parts):
+        for ox, moved in enumerate((pltpu.roll(value, 1, 0), value, pltpu.roll(value, 15, 0))):
+            if f < 2:
+                shifted[f, ox, b, 16 * y + 16 : 16 * y + 32, lanes] = moved.astype(BF16)
+            if y <= 16:
+                key = (f, ox, b, v)
+                before = last_own[key] if y > 0 else jnp.zeros((8, 128), F32)
+                last_own[key] = moved[0:8]
+                at = 8 * (y - 1) if y % 2 == 1 else 128 + 8 * y
+                packed[f, ox, b, at : at + 16, lanes] = jnp.concatenate([before, moved[0:8]], axis=0).astype(BF16)
+
+    def put_all(f, y, parts):
         for b in range(3):
             lo, hi = parts[b]
             lo = jnp.where(group == 0, pltpu.roll(parts[b - 1][1], 64, 1) if b > 0 else 0.0, lo)
             hi = jnp.where(group == 3, pltpu.roll(parts[b + 1][0], 64, 1) if b < 2 else 0.0, hi)
-            put(f, b, 0, r0, lo)
-            put(f, b, 1, r0, hi)
+            put(f, b, 0, y, lo)
+            put(f, b, 1, y, hi)
+
+    def own_inputs(f, ox, oy, y0, ny):
+        at = 8 * y0 + (128 if oy == 0 else 0 if oy == 1 else 144)
+        return packed[f, ox, :, at : at + 8 * ny].reshape(24 * ny, 256)
 
     def inputs_of(f, ox, oy, ny):
         return shifted[f, ox, :, 16 * oy : 16 * oy + 16 * ny].reshape(48 * ny, 256)
 
-    def conv(f, slot, back, y0, ny):
+    def conv(f, y0, ny):
         lhs = jnp.concatenate([inputs_of(f, ox, y0 + oy, ny) for ox in range(3) for oy in range(3)], axis=1)
-        if back:
-            rhs, dims = jnp.concatenate([bands[slot, t] for t in range(9)], axis=1), NT
-        else:
-            rhs, dims = bands[slot].reshape(9 * 256, 256), NN
-        pre[slot, :, 16 * y0 : 16 * y0 + 16 * ny] = dot(lhs, rhs, dims).reshape(3, 16 * ny, 256)
+        pre[f, :, 16 * y0 : 16 * y0 + 16 * ny] = dot(lhs, bands[f].reshape(9 * 256, 256)).reshape(3, 16 * ny, 256)
+
+    def conv_back(f, slot, y0, ny):
+        lhs = jnp.concatenate([own_inputs(f, ox, oy, y0, ny) for ox in range(3) for oy in range(3)], axis=1)
+        rhs = jnp.concatenate([bands[slot, t] for t in range(9)], axis=1)
+        back[f - 2, :, 8 * y0 : 8 * y0 + 8 * ny] = dot(lhs, rhs, NT).reshape(3, 8 * ny, 256)
 
     def send_rows(f, rows):
         square = ones_at(iota((216, 216), 0) == iota((216, 216), 1))
         four = jnp.concatenate([rows[...]] * 4, axis=0)
         full = jnp.concatenate([dot(square, four, NT), jnp.zeros((8, 128), F32)], axis=0)
-        packed = pick(group, [full[56 * g : 56 * g + 56] for g in range(4)])
-        packed = jnp.concatenate([packed, jnp.zeros((8, 128), F32)], axis=0).astype(BF16)
-        wsend[f] = packed
-        wrecv[f, dp] = packed
+        lined = pick(group, [full[56 * g : 56 * g + 56] for g in range(4)])
+        lined = jnp.concatenate([lined, jnp.zeros((8, 128), F32)], axis=0).astype(BF16)
+        wsend[f] = lined
+        wrecv[f, dp] = lined
 
     def share_rows(f):
         sems = (filt_send, filt_recv)
@@ -296,8 +317,7 @@
                         bands[2 + f, 3 * sx + sy, C * zo : C * zo + C, 128 * v : 128 * v + 128] = value
 
     def natural(blocked):
-        rows = jnp.concatenate([dot(pack[...], blocked[b]) for b in range(3)], axis=1).astype(BF16)
-        return dot(rows, unplace[...])
+        return dot(jnp.concatenate([blocked[b] for b in range(3)], axis=1), unplace[...])
 
     def depart(field, out):
         for w in range(4):
@@ -312,10 +332,10 @@
         out[0, 0] = dot(cells, turn[...]).reshape(C, 8, 256).astype(BF16)
 
     def filter_gradient(f, r):
-        gradient = owned[f].reshape(768, 256)
+        gradient = owned[f].reshape(384, 256)
         odd, high = group % 2 == 1, group >= 2
         for t in range(9):
-            product[f, t] = dot(gradient, inputs_of(r, t // 3, t % 3, 16), TN)
+            product[f, t] = dot(gradient, own_inputs(r, t // 3, t % 3, 0, 16), TN)
             for oz in range(3):
                 a = []
                 for j in range(4):
@@ -352,13 +372,14 @@
     field = jnp.where(kept_cells > 0.5, vin[...].astype(F32).reshape(256, 256), GONE)
     field = turn_in(0, field)
     show(0, 3, sel3[...], field)
+    pl.semaphore_wait(barrier, len(greeted))
+    volume_near, volume_far = give(0, 3)
     loads[2].wait()
     loads[3].wait()
     send_rows(0, rows_in.at[0])
+    row_moves = [share_rows(0)]
     send_rows(1, rows_in.at[1])
-    pl.semaphore_wait(barrier, len(greeted))
-    volume_near, volume_far = give(0, 3)
-    row_moves = [share_rows(0), share_rows(1)]
+    row_moves.append(share_rows(1))
 
     near3[...], far3[...] = assemble(3)
     k, n = iota((256, 256), 0), iota((256, 256), 1)
@@ -371,8 +392,6 @@
     show(1, 1, sel1[...], turn_in(1, cin[...].astype(F32).reshape(256, 256)))
     cot_near, cot_far = give(1, 1)
     near1[...], far1[...] = assemble(1)
-    row, col = iota((128, 256), 0), iota((128, 256), 1)
-    pack[...] = ones_at(col == 16 * (row // 8) + row % 8 + 4)
     for b in range(3):
         k, n = iota((256, 640), 0), iota((256, 640), 1)
         zi, z = k // C, 6 * b + k // C - 1
@@ -380,9 +399,9 @@
         unplace[256 * b : 256 * b + 256] = ones_at(
             good & (((n < 512) & (n // C == z)) | ((n >= 544) & (16 - (n // C - 16) == z)))
         )
-    x = iota((304, 128), 0) % 16 - 4
+    x = x_of(iota((304, 128), 0))
     inside[...] = jnp.where(((x < 0) & ~has_below) | ((x >= 8) & ~has_above), 0.0, 1.0)
-    for f in range(4):
+    for f in range(2):
         for ox in range(3):
             for b in range(3):
                 shifted[f, ox, b, 0:16] = jnp.zeros((16, 256), BF16)
@@ -405,7 +424,7 @@
                 value = blk[b, rows, lanes]
                 kept_here = jnp.where(value == GONE, 0.0, here)
                 keep[b, rows, lanes] = kept_here
-                put(0, b, v, 16 * y, value * kept_here)
+                put(0, b, v, y, value * kept_here)
 
     def second(y):
         rows = slice(16 * y, 16 * y + 16)
@@ -414,14 +433,12 @@
             value, there = pre[0, b, rows, :], keep[b, rows, :]
             gate = logistic(value)
             act = value * gate
-            slope[b, rows, :] = (gate + act * (1.0 - gate)) * there
+            if y < 16:
+                slope[b, 8 * y : 8 * y + 8, :] = ((gate + act * (1.0 - gate)) * there)[0:8]
             parts.append(halves(act * there))
-        put_all(1, 16 * y, parts)
-
-    x = iota((16, 128), 0) - 4
-    own = [jnp.where((x >= 0) & (x < 8), 1.0, 0.0)]
-    own.append(jnp.where(group == 0, own[0], 0.0))
-    own_lanes = [jnp.concatenate([own[0], own[b // 2]], axis=1) for b in range(3)]
+        put_all(1, y, parts)
+
+    own_lanes = [1.0, 1.0, jnp.where(iota((1, 256), 1) < 160, 1.0, 0.0)]
 
     def third(y):
         rows = slice(16 * y, 16 * y + 16)
@@ -433,43 +450,45 @@
             grad = cot[b, rows, :] * there * (gate + act * (1.0 - gate))
             parts.append(halves(grad))
             if y < 16:
-                leaving[b, rows, :] = (act * there).astype(BF16)
-                owned[1, b, rows, :] = (grad * own_lanes[b]).astype(BF16)
-        put_all(2, 16 * y, parts)
+                key, mine = ("own", b), ((act * there)[0:8], (grad * own_lanes[b])[0:8])
+                if y % 2 == 1:
+                    pair = [jnp.concatenate(p, axis=0).astype(BF16) for p in zip(last_own[key], mine)]
+                    leaving[b, 8 * y - 8 : 8 * y + 8, :] = pair[0]
+                    owned[1, b, 8 * y - 8 : 8 * y + 8, :] = pair[1]
+                last_own[key] = mine
+        put_all(2, y, parts)
 
     def fourth(y):
-        rows = slice(16 * y, 16 * y + 16)
+        rows = slice(8 * y, 8 * y + 16)
         for b in range(3):
-            owned[0, b, rows, :] = (pre[3, b, rows, :] * slope[b, rows, :] * own_lanes[b]).astype(BF16)
-
-    def run(body, first_y, end):
-        for y in range(first_y, end):
+            owned[0, b, rows, :] = (back[0, b, rows, :] * slope[b, rows, :] * own_lanes[b]).astype(BF16)
+
+    def run(body, first_y, end, step=1):
+        for y in range(first_y, end, step):
             body(y)
 
     run(first, 0, 8)
-    conv(0, 0, False, 0, 6)
+    conv(0, 0, 6)
     run(first, 8, 16)
-    conv(0, 0, False, 6, 6)
+    conv(0, 6, 6)
     run(second, 0, 6)
     take(0, 3, far3, 1, volume_far, blk)
     run(first, 16, 19)
-    conv(0, 0, False, 12, 6)
+    conv(0, 12, 6)
     run(second, 6, 12)
-    conv(1, 1, False, 0, 6)
+    conv(1, 0, 6)
     run(second, 12, 18)
-    conv(1, 1, False, 6, 6)
+    conv(1, 6, 6)
     take(1, 1, near1, 0, cot_near, cot)
     run(third, 0, 6)
-    conv(1, 1, False, 12, 5)
+    conv(1, 12, 5)
     run(third, 6, 12)
-    conv(2, 3, True, 0, 6)
     run(third, 12, 16)
+    conv_back(2, 3, 0, 8)
     take(1, 1, far1, 1, cot_far, cot)
     run(third, 16, 17)
-    conv(2, 3, True, 6, 5)
-    run(fourth, 0, 6)
-    conv(2, 3, True, 11, 5)
-    run(fourth, 6, 16)
+    conv_back(2, 3, 8, 8)
+    run(fourth, 0, 16, 2)
     pair_one = filter_gradient(0, 0)
     pair_two = filter_gradient(1, 1)
     show(2, 1, sel1[...], natural(owned[0]).astype(BF16))
@@ -501,22 +520,20 @@
         here = inside[rows, :]
         for b in range(3):
             for v in range(2):
-                put(3, b, v, 16 * y, blk[b, rows, 128 * v : 128 * v + 128] * here)
+                put(3, b, v, y, blk[b, rows, 128 * v : 128 * v + 128] * here)
 
     def sixth(y):
-        rows = slice(16 * y, 16 * y + 16)
+        rows = slice(8 * y, 8 * y + 16)
         for b in range(3):
-            leaving[b, rows, :] = (pre[2, b, rows, :] * keep[b, rows, :]).astype(BF16)
-
-    run(fifth, 0, 8)
-    conv(3, 2, True, 0, 6)
-    run(fifth, 8, 16)
-    conv(3, 2, True, 6, 5)
-    run(sixth, 0, 6)
+            there = [keep[b, 16 * i : 16 * i + 8, :] for i in (y, y + 1)]
+            leaving[b, rows, :] = (back[1, b, rows, :] * jnp.concatenate(there, axis=0)).astype(BF16)
+
+    run(fifth, 0, 16)
+    conv_back(3, 2, 0, 8)
     take(2, 1, far1, 1, grad_far, blk)
     run(fifth, 16, 17)
-    conv(3, 2, True, 11, 5)
-    run(sixth, 6, 16)
+    conv_back(3, 2, 8, 8)
+    run(sixth, 0, 16, 2)
     depart(natural(leaving[...]), gin_out)
 
     for move in z_moves:
@@ -580,12 +597,14 @@
             blocked,
             blocked,
             blocked,
-            blocked,
-            pltpu.VMEM((4, 3, 288, 256), F32),
-            pltpu.VMEM((4, 3, 3, 320, 256), BF16),
+            pltpu.VMEM((3, 128, 256), F32),
+            pltpu.VMEM((2, 3, 288, 256), F32),
+            pltpu.VMEM((2, 3, 128, 256), F32),
+            pltpu.VMEM((2, 3, 3, 320, 256), BF16),
+            pltpu.VMEM((4, 3, 3, 272, 256), BF16),
             pltpu.VMEM((4, 9, 256, 256), BF16),
-            pltpu.VMEM((3, 256, 256), BF16),
-            pltpu.VMEM((2, 3, 256, 256), BF16),
+            pltpu.VMEM((3, 128, 256), BF16),
+            pltpu.VMEM((2, 3, 128, 256), BF16),
             pltpu.VMEM((256, 1024), BF16),
             pltpu.VMEM((2, 64, 128), BF16),
             pltpu.VMEM((2, 4, 64, 128), BF16),
@@ -611,7 +630,6 @@
             pltpu.VMEM((256, 256), BF16),
             pltpu.VMEM((384, 256), BF16),
             pltpu.VMEM((384, 256), BF16),
-            pltpu.VMEM((128, 256), BF16),
             pltpu.VMEM((768, 640), BF16),
             pltpu.VMEM((304, 128), F32),
             dma((5,)), dma((3, 4)), dma((3, 4)), dma((2,)), dma((2,)),

time: 42.4 us -> 41.6 us (0.981)
  Pallas kernels: 41.6 us -> 40.9 us
    pallas_call x1, Pallas kernels: 40.9 us -> 40.1 us  [on_device(): pl.pallas_call(kernel, out_shape=tuple((pltpu.VMEM(*r) for r in results))...]
where the time goes in v5:
time: 41.6 us; the launch traced here: 41.5 us
  Pallas kernels  40.9 us (98%)
  between operations  0.64 us (2%)
    pallas_call x1, Pallas kernels, on_device(): pl.pallas_call(kernel, out_shape=tuple((pltpu.VMEM(*r) for r in results))...  40.1 us

profile of v5, /device:TPU:1, one launch (start us, length us, event | category | flops | bytes accessed | tf_op | source)
XLA Modules:
  0.0 41.5 jit_solution(6119577953849572855)
XLA Ops:
  0.6 40.1 %shard_map.84 = (bf16[1,1,32,8,256]{4,3,2,1,0:T(8,128)(2,1)S(1)}, bf16[1,1,32,8,256]{4,3,2,1,0:T(8,128)(2,1)S(1)}, f32[32,216]{1,0:T(8,128)S(1)}, f32[32,216]{1,0:T(8,128)S(1)}) custom-call(s32[1,1,4]{2,1,0:T(1,128)} %flags.1, bf16[32,216]{1,0:T(8,128)(2,1)} %bitcast.4, bf16[32,216]{1,0:T(8,128)(2,1)} %bitcast.5, bf16[1,1,32,8,256]{4,3,2,1,0:T(8,128)(2,1)} %volume.1, ...), custom_call_target="tpu_custom_call" | custom-call | tf_op jit(solution)/shard_map/pallas_call | solution.py:579
  40.8 0.7 %shard_map.85 = (bf16[1,1,32,8,256]{4,3,2,1,0:T(8,128)(2,1)}, bf16[1,1,32,8,256]{4,3,2,1,0:T(8,128)(2,1)}, f32[32,216]{1,0:T(8,128)}, f32[32,216]{1,0:T(8,128)}) custom-call(bf16[1,1,32,8,256]{4,3,2,1,0:T(8,128)(2,1)S(1)} %get-tuple-element.12.refs_0_, bf16[1,1,32,8,256]{4,3,2,1,0:T(8,128)(2,1)S(1)} %get-tuple-element.13.refs_1_, ...), custom_call_target="tpu_custom_call" | custom-call | tf_op jit(solution)/shard_map/pallas_call | solution.py:642

commit v6 on v5

--- a/solution.py
+++ b/solution.py
@@ -62,7 +62,7 @@
     act_out, gin_out, grad_one_out, grad_two_out,
     kept, rows_in, vin, cin, spread, nat, nat_main, nat_z, face_main, face_z, stack_main, stack_z,
     blk, cot, keep, slope, pre, back, shifted, packed, bands, leaving, owned, wide,
-    wsend, wrecv, wrows, rep, product, tap_tile, pile, pair_in, crossing, xy_in, z_in, xc_in, final,
+    wsend, wrecv, wrows, rep, product, tap_tile, pair_in, crossing, xy_in, z_in, xc_in, final,
     turn, copies8, sel3, sel1, near3, far3, near1, far1, place0, place1, place2, unplace, inside,
     local_sem, halo_send, halo_recv, filt_send, filt_recv,
     pair_send, pair_recv, xy_send, xy_recv, z_send, z_recv, xc_send, xc_recv,
@@ -331,11 +331,11 @@
         cells = dot(copies8[...], wide[...], NT).astype(BF16)
         out[0, 0] = dot(cells, turn[...]).reshape(C, 8, 256).astype(BF16)
 
-    def filter_gradient(f, r):
+    def filter_gradient(slot, f):
         gradient = owned[f].reshape(384, 256)
         odd, high = group % 2 == 1, group >= 2
         for t in range(9):
-            product[f, t] = dot(gradient, own_inputs(r, t // 3, t % 3, 0, 16), TN)
+            product[slot, t] = dot(gradient, own_inputs(f, t // 3, t % 3, 0, 16), TN)
             for oz in range(3):
                 a = []
                 for j in range(4):
@@ -345,23 +345,15 @@
                         for g in range(4):
                             zo = 4 * v + g - (oz - 1)
                             at = zo * C + 8 * j
-                            parts.append(product[f, t, at : at + 8, 128 * v : 128 * v + 128] if 1 <= zo <= 6 else None)
+                            parts.append(product[slot, t, at : at + 8, 128 * v : 128 * v + 128] if 1 <= zo <= 6 else None)
                         sides.append(pick(group, parts))
                     a.append(sides[0] + sides[1])
                 pairs = [
                     jnp.where(odd, a[i + 1], a[i]) + pltpu.roll(jnp.where(odd, a[i], a[i + 1]), 32, 1) for i in (0, 2)
                 ]
-                tap_tile[f, tap(t // 3, t % 3, oz)] = jnp.where(high, pairs[1], pairs[0]) + pltpu.roll(
+                tap_tile[slot, tap(t // 3, t % 3, oz)] = jnp.where(high, pairs[1], pairs[0]) + pltpu.roll(
                     jnp.where(high, pairs[0], pairs[1]), 64, 1
                 )
-        for q in range(4):
-            for k in range(8):
-                source = STARTS[q] + k
-                pile[f, k // 4, 4 * (k % 4) + q] = (
-                    tap_tile[f, source] if source < 27 else jnp.zeros((8, 128), F32)
-                )
-        send(pile.at[f, 1 - rz], pair_in.at[f], (pair_send, pair_recv), f, (column[2], dp))
-        return batch(pair_in.at[f], (pair_send, pair_recv), f)
 
     loads[0].wait()
     loads[1].wait()
@@ -489,14 +481,17 @@
     run(third, 16, 17)
     conv_back(2, 3, 8, 8)
     run(fourth, 0, 16, 2)
-    pair_one = filter_gradient(0, 0)
-    pair_two = filter_gradient(1, 1)
+    filter_gradient(0, 1 - rz)
+    send(tap_tile.at[0], pair_in, (pair_send, pair_recv), 0, (column[2], dp))
+    pair = batch(pair_in, (pair_send, pair_recv), 0)
+    filter_gradient(1, rz)
     show(2, 1, sel1[...], natural(owned[0]).astype(BF16))
     grad_near, grad_far = give(2, 1)
-    for f, move in ((0, pair_one), (1, pair_two)):
-        move.wait_recv()
-        for s in range(16):
-            crossing[s, f] = pile[f, rz, s] + pair_in[f, s]
+    pair.wait_recv()
+    for s in range(16):
+        for j in range(2):
+            source = STARTS[s % 4] + 2 * (s // 4) + j
+            crossing[s, j] = tap_tile[1, source] + pair_in[source] if source < 27 else jnp.zeros((8, 128), F32)
     for s, peer in zip(xy_slots, xy_peers):
         send(crossing.at[s], xy_in.at[xy], (xy_send, xy_recv), 0, peer)
     xy_moves = [batch(xy_in.at[0:15], (xy_send, xy_recv), 0)]
@@ -553,7 +548,7 @@
             for w in range(2):
                 parts = []
                 for g in range(4):
-                    value = xc_in[4 * w + g].astype(F32)[8 * f : 8 * f + 8]
+                    value = xc_in[4 * f + 2 * w + g // 2].astype(F32)[8 * (g % 2) : 8 * (g % 2) + 8]
                     parts.append(value if g == j else pltpu.roll(value, 32 * ((g - j) % 4), 1))
                 final[8 * j : 8 * j + 8, 128 * w : 128 * w + 128] = pick(group, parts)
         out[...] = pltpu.roll(final[...], 256 - offset, 1)[:, :216]
@@ -612,8 +607,7 @@
             pltpu.VMEM((2, 27, C, 128), F32),
             pltpu.VMEM((2, 9, 256, 256), F32),
             pltpu.VMEM((2, 27, 8, 128), F32),
-            pltpu.VMEM((2, 2, 16, 8, 128), F32),
-            pltpu.VMEM((2, 16, 8, 128), F32),
+            pltpu.VMEM((27, 8, 128), F32),
             pltpu.VMEM((16, 2, 8, 128), F32),
             pltpu.VMEM((16, 2, 8, 128), F32),
             pltpu.VMEM((8, 16, 128), BF16),
@@ -633,7 +627,7 @@
             pltpu.VMEM((768, 640), BF16),
             pltpu.VMEM((304, 128), F32),
             dma((5,)), dma((3, 4)), dma((3, 4)), dma((2,)), dma((2,)),
-            dma((2,)), dma((2,)), dma((1,)), dma((1,)), dma((1,)), dma((1,)), dma((1,)), dma((1,)),
+            dma((1,)), dma((1,)), dma((1,)), dma((1,)), dma((1,)), dma((1,)), dma((1,)), dma((1,)),
         ],
         compiler_params=pltpu.CompilerParams(
             collective_id=0, has_side_effects=True, vmem_limit_bytes=60 * 1024 * 1024

time: 41.6 us -> 41.1 us (0.988)
  Pallas kernels: 40.9 us -> 40.4 us
    pallas_call x1, Pallas kernels: 40.1 us -> 39.6 us  [on_device(): pl.pallas_call(kernel, out_shape=tuple((pltpu.VMEM(*r) for r in results))...]
where the time goes in v6:
time: 41.1 us; the launch traced here: 41 us
  Pallas kernels  40.4 us (98%)
  between operations  0.64 us (2%)
    pallas_call x1, Pallas kernels, on_device(): pl.pallas_call(kernel, out_shape=tuple((pltpu.VMEM(*r) for r in results))...  39.6 us

profile of v6, /device:TPU:1, one launch (start us, length us, event | category | flops | bytes accessed | tf_op | source)
XLA Modules:
  0.0 41.0 jit_solution(11853684103947468812)
XLA Ops:
  0.6 39.6 %shard_map.84 = (bf16[1,1,32,8,256]{4,3,2,1,0:T(8,128)(2,1)S(1)}, bf16[1,1,32,8,256]{4,3,2,1,0:T(8,128)(2,1)S(1)}, f32[32,216]{1,0:T(8,128)S(1)}, f32[32,216]{1,0:T(8,128)S(1)}) custom-call(s32[1,1,4]{2,1,0:T(1,128)} %flags.1, bf16[32,216]{1,0:T(8,128)(2,1)} %bitcast.4, bf16[32,216]{1,0:T(8,128)(2,1)} %bitcast.5, bf16[1,1,32,8,256]{4,3,2,1,0:T(8,128)(2,1)} %volume.1, ...), custom_call_target="tpu_custom_call" | custom-call | tf_op jit(solution)/shard_map/pallas_call | solution.py:574
  40.3 0.7 %shard_map.85 = (bf16[1,1,32,8,256]{4,3,2,1,0:T(8,128)(2,1)}, bf16[1,1,32,8,256]{4,3,2,1,0:T(8,128)(2,1)}, f32[32,216]{1,0:T(8,128)}, f32[32,216]{1,0:T(8,128)}) custom-call(bf16[1,1,32,8,256]{4,3,2,1,0:T(8,128)(2,1)S(1)} %get-tuple-element.12.refs_0_, bf16[1,1,32,8,256]{4,3,2,1,0:T(8,128)(2,1)S(1)} %get-tuple-element.13.refs_1_, ...), custom_call_target="tpu_custom_call" | custom-call | tf_op jit(solution)/shard_map/pallas_call | solution.py:636

commit v7 on v6

--- a/solution.py
+++ b/solution.py
@@ -116,7 +116,7 @@
     dp_peers = [(space, lax.rem(dp + k, 4)) for k in range(1, 4)]
 
     barrier = pltpu.get_barrier_semaphore()
-    greeted = [(d, dp) for d in column[1:]] + [(d, dp) for d in below + above] + xy_peers + z_peers + xc_peers
+    greeted = [(column[3], dp)] + [(d, dp) for d in below + above] + xy_peers + z_peers + xc_peers
     for peer in greeted:
         pl.semaphore_signal(barrier, inc=1, device_id=peer, device_id_type=MESH)
 
@@ -379,10 +379,6 @@
     k, n = iota((384, 256), 0), iota((384, 256), 1)
     place1[...] = ones_at(k - n == C)
     place2[...] = ones_at(k - n == jnp.where(n < 160, 96, 128))
-    sel1[...] = faces_of(1)
-    loads[4].wait()
-    show(1, 1, sel1[...], turn_in(1, cin[...].astype(F32).reshape(256, 256)))
-    cot_near, cot_far = give(1, 1)
     near1[...], far1[...] = assemble(1)
     for b in range(3):
         k, n = iota((256, 640), 0), iota((256, 640), 1)
@@ -398,6 +394,10 @@
             for b in range(3):
                 shifted[f, ox, b, 0:16] = jnp.zeros((16, 256), BF16)
 
+    sel1[...] = faces_of(1)
+    loads[4].wait()
+    show(1, 1, sel1[...], turn_in(1, cin[...].astype(F32).reshape(256, 256)))
+    cot_near, cot_far = give(1, 1)
     for f in range(2):
         for move in row_moves[f]:
             move.wait_recv()

time: 41.1 us -> 41.1 us (level)
  no operation moved by 1% of the time
where the time goes in v7:
time: 41.1 us; the launch traced here: 41 us
  Pallas kernels  40.3 us (98%)
  between operations  0.64 us (2%)
    pallas_call x1, Pallas kernels, on_device(): pl.pallas_call(kernel, out_shape=tuple((pltpu.VMEM(*r) for r in results))...  39.6 us

profile of v7, /device:TPU:1, one launch (start us, length us, event | category | flops | bytes accessed | tf_op | source)
XLA Modules:
  0.0 41.0 jit_solution(15697671168987611610)
XLA Ops:
  0.6 39.6 %shard_map.84 = (bf16[1,1,32,8,256]{4,3,2,1,0:T(8,128)(2,1)S(1)}, bf16[1,1,32,8,256]{4,3,2,1,0:T(8,128)(2,1)S(1)}, f32[32,216]{1,0:T(8,128)S(1)}, f32[32,216]{1,0:T(8,128)S(1)}) custom-call(s32[1,1,4]{2,1,0:T(1,128)} %flags.1, bf16[32,216]{1,0:T(8,128)(2,1)} %bitcast.4, bf16[32,216]{1,0:T(8,128)(2,1)} %bitcast.5, bf16[1,1,32,8,256]{4,3,2,1,0:T(8,128)(2,1)} %volume.1, ...), custom_call_target="tpu_custom_call" | custom-call | tf_op jit(solution)/shard_map/pallas_call | solution.py:574
  40.2 0.7 %shard_map.85 = (bf16[1,1,32,8,256]{4,3,2,1,0:T(8,128)(2,1)}, bf16[1,1,32,8,256]{4,3,2,1,0:T(8,128)(2,1)}, f32[32,216]{1,0:T(8,128)}, f32[32,216]{1,0:T(8,128)}) custom-call(bf16[1,1,32,8,256]{4,3,2,1,0:T(8,128)(2,1)S(1)} %get-tuple-element.12.refs_0_, bf16[1,1,32,8,256]{4,3,2,1,0:T(8,128)(2,1)S(1)} %get-tuple-element.13.refs_1_, ...), custom_call_target="tpu_custom_call" | custom-call | tf_op jit(solution)/shard_map/pallas_call | solution.py:636
